TPU v7x, 256 devices: a whole 4x4x8 slice. The times are simulated.
256 devices in a mesh: bond: 16 (over z, core), sec: 16 (over y, x).
Axes of the slice: x: 4, y: 4, z: 8, core: 2. Of those that a mesh axis runs over, the one named last changes fastest.
Arguments:
- left_site: bfloat16 [16, 64, 512, 512], P('bond', 'sec'), may hold values from -6 to 6
- right_site: bfloat16 [16, 64, 512, 512], P('bond', 'sec'), may hold values from -0.25 to 0.25
- gate: float32 [64, 64], replicated, may hold values from -2 to 2
- sign_table: int32 [64, 64], replicated, may hold values 0 or 1
- kept: int32 [16, 64], P('bond', 'sec'), may hold values from 32 to 128, as said below
- start: float32 [16, 64, 512, 128], P('bond', 'sec'), may hold values from -6 to 6
Outputs:
- left_new: bfloat16 [16, 64, 512, 128], P('bond', 'sec')
- right_new: bfloat16 [16, 64, 128, 512], P('bond', 'sec')
Inputs may be any that keep to these rules, and one draw needn't show every extreme that they name: `kept`: kept counts are largest on the central bonds; sector 0 of bond 16 // 2 keeps 128.
All inputs are finite; a program needn't handle non-finite values.
Results may differ from a plain program's by a relative error of at most 0.011.
Values may be sent and summed in bfloat16 or wider, within the bound.
A program may use at most 64 MiB of HBM per device.

v0:
```python
import jax
import jax.numpy as jnp
from jax import lax
from jax.sharding import PartitionSpec as P

ITERS = 4


def shifted(value, axis, by):
    peers = lax.axis_size(axis)
    return lax.ppermute(value, axis, [(i, (i + by) % peers) for i in range(peers)])


def from_behind(value, axis, steps):
    count = lax.axis_size(axis)
    initial, last = (max(0, -steps), min(count, count - steps))
    return lax.ppermute(value, axis, [(source, source + steps) for source in range(initial, last)])


def shards(left_site, right_site, gate, sign_table, kept, start):
    sec_count = left_site.shape[1]
    block = left_site.shape[2]
    kmax = start.shape[3]
    sectors = gate.shape[0]
    sec_index = lax.axis_index("sec")
    index = jnp.arange(sectors, dtype=jnp.int32)
    first = index // sec_count
    second = index % sec_count
    allowed = (jnp.abs(first[:, None] - first[None, :]) <= 1) & (
        jnp.abs(second[:, None] - second[None, :]) <= 1
    )
    coef = jnp.where(allowed, gate * (1.0 - 2.0 * sign_table.astype(jnp.float32)), jnp.float32(0.0))
    partner = shifted(right_site, "bond", -1)
    pair = jnp.einsum(
        "qij,qjk->qik", left_site[0], partner[0], preferred_element_type=jnp.float32
    ).astype(jnp.bfloat16)
    flat = pair.reshape(sec_count, block * block)
    own_columns = lax.dynamic_slice_in_dim(coef, sec_index * sec_count, sec_count, 1)
    padded = jnp.pad(own_columns, ((sec_count, sec_count), (0, 0)))
    weights = lax.dynamic_slice_in_dim(padded, sec_index * sec_count, 3 * sec_count, 0)
    contrib = jnp.dot(weights, flat.astype(jnp.float32), precision=lax.Precision.HIGHEST)
    from_below = from_behind(contrib[2 * sec_count :], "sec", 1)
    from_above = from_behind(contrib[:sec_count], "sec", -1)
    mixed = contrib[sec_count : 2 * sec_count] + from_below + from_above
    theta = mixed.astype(jnp.bfloat16).reshape(sec_count, block, block)
    gram = jnp.einsum("pij,pkj->pik", theta, theta, preferred_element_type=jnp.float32)
    basis = start[0]
    for step in range(ITERS):
        grown = jnp.einsum("pij,pjk->pik", gram, basis, precision=lax.Precision.HIGHEST)
        inner = jnp.einsum("pji,pjk->pik", grown, grown, precision=lax.Precision.HIGHEST)
        factor = jnp.linalg.cholesky(inner)
        basis = lax.linalg.triangular_solve(
            factor, grown, left_side=False, lower=True, transpose_a=True
        )
    column = jnp.arange(kmax, dtype=jnp.int32)
    masked = jnp.where(column[None, None, :] < kept[0][:, None, None], basis, jnp.float32(0.0))
    right_local = jnp.einsum(
        "pik,pij->pkj", masked, theta.astype(jnp.float32), precision=lax.Precision.HIGHEST
    )
    right_local = right_local.astype(jnp.bfloat16)[None]
    right_new = shifted(right_local, "bond", 1)
    return (masked.astype(jnp.bfloat16)[None], right_new)


def solution(mesh):
    return jax.shard_map(
        shards,
        mesh=mesh,
        in_specs=(
            P("bond", "sec", None, None),
            P("bond", "sec", None, None),
            P(),
            P(),
            P("bond", "sec"),
            P("bond", "sec", None, None),
        ),
        out_specs=(P("bond", "sec", None, None), P("bond", "sec", None, None)),
        check_vma=False,
    )
```

profile of v0, /device:TPU:24, one launch (start us, length us, event | category | flops | bytes accessed | tf_op | source)
XLA Modules:
  0.0 540.4 jit_solution(11473285445282857532)
XLA Ops:
  0.6 5.3 collective-permute-start
  7.0 22.8 %collective-permute-done = bf16[1,4,512,512]{3,2,1,0:T(8,128)(2,1)} collective-permute-done((bf16[1,4,512,512]{3,2,1,0:T(8,128)(2,1)}, bf16[1,4,512,512]{3,2,1,0:T(8,128)(2,1)}, u32[]{:S(2)}, u32[]{:S(2)}) %collective-permute-start) | collective-permute-done | bytes 2097184 | tf_op jit(solution)/shard_map/ppermute | solution.py:11
  29.8 2.8 convert_bitcast_fusion
  32.7 1.6 copy.33
  34.3 6.7 %fusion.36 = f32[12,262144]{1,0:T(8,128)S(1)} fusion(bf16[4,262144]{1,0:T(4,128)(2,1)S(1)} %bitcast.100, s32[]{:T(128)S(6)} %select_n.49, f32[64,4]{1,0:T(8,128)S(1)} %fusion.32), kind=kOutput, calls=%fused_computation.54 | convolution fusion | flops 150994944 | bytes 14681092 | tf_op jit(solution)/shard_map/dot_general | solution.py:41
  41.0 2.5 fusion.39
  43.5 3.4 collective-permute-start.1
  46.9 4.8 collective-permute-start.2
  51.8 85.3 %collective-permute-done.1 = f32[4,262144]{1,0:T(4,128)S(1)} collective-permute-done((f32[4,262144]{1,0:T(4,128)}, f32[4,262144]{1,0:T(4,128)S(1)}, u32[]{:S(2)}, u32[]{:S(2)}) %collective-permute-start.1) | collective-permute-done | bytes 4194336 | tf_op jit(solution)/shard_map/ppermute | solution.py:17
  138.0 2.0 fusion.1
  140.1 1.4 fusion.4
  141.6 1.9 copy-done.2
  143.5 3.7 fusion.22
  147.2 1.8 fusion.40
  149.2 46.9 %custom-call.12 = f32[4,128,128]{2,1,0:T(8,128)S(1)} custom-call(f32[4,128,128]{2,1,0:T(8,128)S(1)} %fusion.31), custom_call_target="Cholesky" | custom-call | tf_op jit(solution)/shard_map/jit(cholesky)/cholesky | solution.py:51
  196.3 39.7 %custom-call.13 = f32[4,1,128,128]{2,3,1,0:T(8,128)S(1)} custom-call(f32[4,1,128,128]{3,2,1,0:T(8,128)S(1)} %select_bitcast_fusion.3), custom_call_target="InvertDiagBlocksLowerTriangular" | custom-call | tf_op jit(solution)/shard_map/triangular_solve/custom-call.0 | solution.py:52
  237.1 5.5 %fusion.41 = f32[4,512,128]{2,1,0:T(8,128)S(1)} fusion(f32[4,512,512]{2,1,0:T(8,128)} %copy-done.2, f32[4,512,128]{2,1,0:T(8,128)S(1)} %convolution_bitcast_fusion.3), kind=kOutput, calls=%fused_computation.69 | convolution fusion | flops 1610612736 | bytes 6291456 | tf_op jit(solution)/shard_map/pij,pjk->pik/dot_general | solution.py:49
  242.6 1.8 fusion.42
  244.6 46.9 %custom-call.14 = f32[4,128,128]{2,1,0:T(8,128)S(1)} custom-call(f32[4,128,128]{2,1,0:T(8,128)S(1)} %fusion.29), custom_call_target="Cholesky" | custom-call | tf_op jit(solution)/shard_map/jit(cholesky)/cholesky | solution.py:51
  291.8 39.5 %custom-call.15 = f32[4,1,128,128]{2,3,1,0:T(8,128)S(1)} custom-call(f32[4,1,128,128]{3,2,1,0:T(8,128)S(1)} %select_bitcast_fusion.2), custom_call_target="InvertDiagBlocksLowerTriangular" | custom-call | tf_op jit(solution)/shard_map/triangular_solve/custom-call.0 | solution.py:52
  332.3 5.5 %fusion.43 = f32[4,512,128]{2,1,0:T(8,128)S(1)} fusion(f32[4,512,512]{2,1,0:T(8,128)} %copy-done.2, f32[4,512,128]{2,1,0:T(8,128)S(1)} %convolution_bitcast_fusion.2), kind=kOutput, calls=%fused_computation.71 | convolution fusion | flops 1610612736 | bytes 6291456 | tf_op jit(solution)/shard_map/pij,pjk->pik/dot_general | solution.py:49
  337.8 1.8 fusion.44
  339.8 46.9 %custom-call.16 = f32[4,128,128]{2,1,0:T(8,128)S(1)} custom-call(f32[4,128,128]{2,1,0:T(8,128)S(1)} %fusion.27), custom_call_target="Cholesky" | custom-call | tf_op jit(solution)/shard_map/jit(cholesky)/cholesky | solution.py:51
  387.0 39.5 %custom-call.17 = f32[4,1,128,128]{2,3,1,0:T(8,128)S(1)} custom-call(f32[4,1,128,128]{3,2,1,0:T(8,128)S(1)} %select_bitcast_fusion.1), custom_call_target="InvertDiagBlocksLowerTriangular" | custom-call | tf_op jit(solution)/shard_map/triangular_solve/custom-call.0 | solution.py:52
  427.5 5.5 %fusion.45 = f32[4,512,128]{2,1,0:T(8,128)S(1)} fusion(f32[4,512,512]{2,1,0:T(8,128)} %copy-done.2, f32[4,512,128]{2,1,0:T(8,128)S(1)} %convolution_bitcast_fusion.1), kind=kOutput, calls=%fused_computation.73 | convolution fusion | flops 1610612736 | bytes 6291456 | tf_op jit(solution)/shard_map/pij,pjk->pik/dot_general | solution.py:49
  433.1 1.8 fusion.46
  435.1 46.9 %custom-call.18 = f32[4,128,128]{2,1,0:T(8,128)S(1)} custom-call(f32[4,128,128]{2,1,0:T(8,128)S(1)} %fusion.25), custom_call_target="Cholesky" | custom-call | tf_op jit(solution)/shard_map/jit(cholesky)/cholesky | solution.py:51
  482.3 39.6 %custom-call.19 = f32[4,1,128,128]{2,3,1,0:T(8,128)S(1)} custom-call(f32[4,1,128,128]{3,2,1,0:T(8,128)S(1)} %select_bitcast_fusion), custom_call_target="InvertDiagBlocksLowerTriangular" | custom-call | tf_op jit(solution)/shard_map/triangular_solve/custom-call.0 | solution.py:52
  521.8 1.1 fusion.15
  522.9 3.1 fusion.19
  527.2 11.0 %collective-permute-done.3 = bf16[1,4,128,512]{3,2,1,0:T(8,128)(2,1)} collective-permute-done((bf16[1,4,128,512]{3,2,1,0:T(8,128)(2,1)S(1)}, bf16[1,4,128,512]{3,2,1,0:T(8,128)(2,1)}, u32[]{:S(2)}, u32[]{:S(2)}) %collective-permute-start.3) | collective-permute-done | bytes 524320 | tf_op jit(solution)/shard_map/ppermute | solution.py:11
  538.1 1.9 copy.48
  (45 shorter events, 7.9 us)
Async XLA Ops:
  0.6 29.2 %copy-start = (bf16[1,4,512,512]{3,2,1,0:T(8,128)(2,1)S(1)}, bf16[1,4,512,512]{3,2,1,0:T(8,128)(2,1)}, u32[]{:S(2)}) copy-start(bf16[1,4,512,512]{3,2,1,0:T(8,128)(2,1)} %param.9) | copy-start | bytes 6291460
  0.6 29.2 %collective-permute-start = (bf16[1,4,512,512]{3,2,1,0:T(8,128)(2,1)}, bf16[1,4,512,512]{3,2,1,0:T(8,128)(2,1)}, u32[]{:S(2)}, u32[]{:S(2)}) collective-permute-start(bf16[1,4,512,512]{3,2,1,0:T(8,128)(2,1)} %param.10), channel_id=1, source_target_pairs={{0,240},{16,0},{32,16},{48,32},{64,48},{80,64},{96,80},{112,96},{1... | collective-permute-start | bytes 6291464 | tf_op jit(solution)/shard_map/ppermute | solution.py:11
  41.0 10.7 %copy-start.5 = (s32[1,4]{1,0:T(1,128)S(1)}, s32[1,4]{1,0:T(1,128)}, u32[]{:S(2)}) copy-start(s32[1,4]{1,0:T(1,128)} %param.13) | copy-start | bytes 52
  43.5 93.6 %collective-permute-start.1 = (f32[4,262144]{1,0:T(4,128)}, f32[4,262144]{1,0:T(4,128)S(1)}, u32[]{:S(2)}, u32[]{:S(2)}) collective-permute-start(f32[4,262144]{1,0:T(4,128)} %get-tuple-element.8), channel_id=1, source_target_pairs={{0,1},{1,2},{2,3},{3,4},{4,5},{5,6},{6,7},{7,8},{8,9},{9,10},{10,1... | collective-permute-start | bytes 12582920 | tf_op jit(solution)/shard_map/ppermute | solution.py:17
  46.9 91.2 %collective-permute-start.2 = (f32[4,262144]{1,0:T(4,128)S(1)}, f32[4,262144]{1,0:T(4,128)S(1)}, u32[]{:S(2)}, u32[]{:S(2)}) collective-permute-start(f32[4,262144]{1,0:T(4,128)S(1)} %get-tuple-element.9), channel_id=1, source_target_pairs={{1,0},{2,1},{3,2},{4,3},{5,4},{6,5},{7,6},{8,7},{9,8},{10,9},{11,1... | collective-permute-start | bytes 12582920 | tf_op jit(solution)/shard_map/ppermute | solution.py:17
  140.1 1.5 copy-start.3
  140.1 3.4 copy-start.4
  141.6 1.9 copy-start.2
  521.8 18.1 %copy-start.1 = (bf16[1,4,512,512]{3,2,1,0:T(8,128)(2,1)S(1)}, bf16[1,4,512,512]{3,2,1,0:T(8,128)(2,1)}, u32[]{:S(2)}) copy-start(bf16[1,4,512,512]{3,2,1,0:T(8,128)(2,1)} %param.9) | copy-start | bytes 6291460
  526.0 12.1 %collective-permute-start.3 = (bf16[1,4,128,512]{3,2,1,0:T(8,128)(2,1)S(1)}, bf16[1,4,128,512]{3,2,1,0:T(8,128)(2,1)}, u32[]{:S(2)}, u32[]{:S(2)}) collective-permute-start(bf16[1,4,128,512]{3,2,1,0:T(8,128)(2,1)S(1)} %fusion.19), channel_id=1, source_target_pairs={{0,16},{16,32},{32,48},{48,64},{64,80},{80,96},{96,112},{112,128},... | collective-permute-start | bytes 1572872 | tf_op jit(solution)/shard_map/ppermute | solution.py:11
where the time goes:
time: 550 us; the launch traced here: 540 us
  other arithmetic  350 us (64%)
  waiting for transfers between devices  120 us (22%)
  matrix products  45.7 us (8%)
  starting transfers between devices  13.5 us (2%)
  local copies, waits for them, and re-layouts  9.6 us (2%)
    another operation x13, other arithmetic, shards(): factor = jnp.linalg.cholesky(inner)  188 us
    another operation x9, other arithmetic, shards(): lax.linalg.triangular_solve(factor, grown, left_side=False, lower=True, t...  159 us
    ppermute x2, waiting for transfers between devices, from_behind(): lax.ppermute(value, axis, [(source, source + steps) for source in range(i...  86.3 us
    ppermute x2, waiting for transfers between devices, shifted(): lax.ppermute(value, axis, [(i, (i + by) % peers) for i in range(peers)])  33.8 us
    dot_general x4, matrix products, shards(): jnp.einsum('pij,pjk->pik', gram, basis, precision=lax.Precision.HIGHEST)  20.3 us
  transfers between devices with their start and end apart: 4, of which 4 were waited for; matrix products, arithmetic and copies ran while one was open for 0% of the time, Pallas kernels for 0%

commit v1 on v0

v1 whole, which is shorter than its diff:
```python
import functools
import jax
import jax.numpy as jnp
from jax import lax
from jax.experimental import pallas as pl
from jax.experimental.pallas import tpu as pltpu
from jax.sharding import PartitionSpec as P

ITERS=4
NB=16
F32=jnp.float32; BF=jnp.bfloat16

def split3(x):
    h=x.astype(BF)
    r=x-h.astype(F32)
    m=r.astype(BF)
    l=(r-m.astype(F32)).astype(BF)
    return h,m,l

def dot(a,b,ca,cb):
    return lax.dot_general(a,b,(((ca,),(cb,)),((),())),preferred_element_type=F32)

def dot6(a,b,ca,cb):
    ah,am,al=split3(a); bh,bm,bl=split3(b)
    return (dot(ah,bh,ca,cb)+(dot(ah,bm,ca,cb)+dot(am,bh,ca,cb))
            +(dot(ah,bl,ca,cb)+dot(am,bm,ca,cb)+dot(al,bh,ca,cb)))

def factor(aug, ubuf, tri, n, nb, S):
    for t in range(n//nb):
        lo=t*nb
        X=[aug[pl.ds(lo+k,2*S,stride=n),:] for k in range(nb)]
        v={}
        for i in range(nb):
            xa=jnp.concatenate([X[i][:S],X[i][:S]],axis=0)
            for k in range(i+1):
                v[i,k]=jnp.broadcast_to(xa[:,lo+k:lo+k+1],(2*S,n))
        U=[None]*nb
        for j in range(nb):
            r=lax.rsqrt(v[j,j])
            U[j]=X[j]*r
            tri[pl.ds(lo+j,S,stride=n),:]=U[j][S:]
            ubuf[pl.ds(j,2*S,stride=nb),:]=U[j]
            col={}
            for i in range(j+1,nb):
                col[i]=v[i,j]*r
            for i in range(j+1,nb):
                for k in range(j+1,i+1):
                    v[i,k]=v[i,k]-col[i]*col[k]
                X[i]=X[i]-col[i]*U[j]
        if lo+nb<n:
            for s in range(S):
                h,m,l=split3(ubuf[s*nb:(s+1)*nb,:])
                lhs=jnp.concatenate([h,h,m,h,m,l],axis=0)
                rhs=jnp.concatenate([h,m,h,l,m,h],axis=0)
                h,m,l=split3(ubuf[(S+s)*nb:(S+s+1)*nb,:])
                rhs2=jnp.concatenate([h,m,h,l,m,h],axis=0)
                up=dot(lhs,jnp.concatenate([rhs,rhs2],axis=1),0,0)
                rows=slice(s*n+lo+nb,(s+1)*n)
                aug[rows,:]=aug[rows,:]-up[lo+nb:,:n]
                rows=slice((S+s)*n+lo+nb,(S+s+1)*n)
                aug[rows,:]=aug[rows,:]-up[lo+nb:,n:]

def body(theta, start, kept, left, right, bt, gt, aug, ubuf, tri):
    S=theta.shape[0]; n=start.shape[2]; d=theta.shape[1]
    eye=(lax.broadcasted_iota(jnp.int32,(n,n),0)==lax.broadcasted_iota(jnp.int32,(n,n),1)).astype(F32)
    for s in range(S):
        bt[s]=start[s].T
    def it(_,c):
        for s in range(S):
            h,m,l=split3(bt[s])
            th=theta[s]
            z=dot(h,th,1,0)+(dot(m,th,1,0)+dot(l,th,1,0))
            h,m,l=split3(z)
            g=dot(h,th,1,1)+(dot(m,th,1,1)+dot(l,th,1,1))
            gt[s]=g
            aug[s*n:(s+1)*n,:]=dot6(g,g,1,1)
            aug[(S+s)*n:(S+s+1)*n,:]=eye
        factor(aug,ubuf,tri,n,NB,S)
        for s in range(S):
            bt[s]=dot6(tri[s*n:(s+1)*n,:],gt[s],1,0)
        return c
    lax.fori_loop(0,ITERS,it,0)
    for s in range(S):
        row=lax.broadcasted_iota(jnp.int32,(n,d),0)
        masked=jnp.where(row<kept[0,s],bt[s],0.0)
        left[s]=masked.T.astype(BF)
        h,m,l=split3(masked)
        th=theta[s]
        right[s]=(dot(h,th,1,0)+(dot(m,th,1,0)+dot(l,th,1,0))).astype(BF)

def subspace(theta,start,kept):
    S,d,_=theta.shape; n=start.shape[2]
    return pl.pallas_call(body,
        out_shape=(jax.ShapeDtypeStruct((S,d,n),BF),jax.ShapeDtypeStruct((S,n,d),BF)),
        in_specs=[pl.BlockSpec(memory_space=pltpu.VMEM),pl.BlockSpec(memory_space=pltpu.VMEM),pl.BlockSpec(memory_space=pltpu.SMEM)],
        out_specs=[pl.BlockSpec(memory_space=pltpu.VMEM)]*2,
        scratch_shapes=[pltpu.VMEM((S,n,d),F32),pltpu.VMEM((S,n,d),F32),pltpu.VMEM((2*S*n,n),F32),pltpu.VMEM((2*S*NB,n),F32),pltpu.VMEM((S*n,n),F32)],
        compiler_params=pltpu.CompilerParams(vmem_limit_bytes=40*2**20),
    )(theta,start,kept)


def shifted(value, axis, by):
    peers = lax.axis_size(axis)
    return lax.ppermute(value, axis, [(i, (i + by) % peers) for i in range(peers)])


def from_behind(value, axis, steps):
    count = lax.axis_size(axis)
    initial, last = (max(0, -steps), min(count, count - steps))
    return lax.ppermute(value, axis, [(source, source + steps) for source in range(initial, last)])


def shards(left_site, right_site, gate, sign_table, kept, start):
    sec_count = left_site.shape[1]
    sectors = gate.shape[0]
    sec_index = lax.axis_index("sec")
    coef = gate * (1.0 - 2.0 * sign_table.astype(jnp.float32))
    padded = jnp.pad(coef, ((0, 0), (sec_count, sec_count)))
    rows = lax.dynamic_slice_in_dim(padded, sec_index * sec_count, sec_count, 0)
    weights = lax.dynamic_slice_in_dim(rows, sec_index * sec_count, 3 * sec_count, 1)
    partner = shifted(right_site, "bond", -1)
    pair = jnp.einsum(
        "qij,qjk->qik", left_site[0], partner[0], preferred_element_type=jnp.float32
    ).astype(jnp.bfloat16)
    below = from_behind(pair, "sec", 1)
    above = from_behind(pair, "sec", -1)
    theta = []
    for p in range(sec_count):
        total = None
        for c, block in enumerate((below, pair, above)):
            for q in range(max(0, p - 1), min(sec_count, p + 2)):
                term = weights[p, c * sec_count + q] * block[q].astype(jnp.float32)
                total = term if total is None else total + term
        theta.append(total.astype(jnp.bfloat16))
    theta = jnp.stack(theta)
    left_new, right_local = subspace(theta, start[0], kept)
    return (left_new[None], shifted(right_local[None], "bond", 1))


def solution(mesh):
    return jax.shard_map(
        shards,
        mesh=mesh,
        in_specs=(
            P("bond", "sec", None, None),
            P("bond", "sec", None, None),
            P(),
            P(),
            P("bond", "sec"),
            P("bond", "sec", None, None),
        ),
        out_specs=(P("bond", "sec", None, None), P("bond", "sec", None, None)),
        check_vma=False,
    )
```

time: 550 us -> 174 us (0.32); the launches traced: 540 us -> 173 us
  other arithmetic: 350 us -> 30.4 us
  Pallas kernels: 0 us -> 43.6 us
  matrix products: 45.7 us -> 2.6 us
  waiting for transfers between devices: 120 us -> 80.5 us
  local copies, waits for them, and re-layouts: 9.6 us -> 3.25 us
    another operation x22 -> x1, other arithmetic: 347 us -> 0.26 us  [shards(): theta = jnp.stack(theta)]
    pallas_call x0 -> x1, Pallas kernels: none -> 43.6 us  [subspace(): pl.pallas_call(body, out_shape=(jax.ShapeDtypeStruct((S, d, n), BF), jax....]
    ppermute x2, waiting for transfers between devices: 86.3 us -> 44.9 us  [from_behind(): lax.ppermute(value, axis, [(source, source + steps) for source in range(i...]
    dot_general x11 -> x0, matrix products: 38.8 us -> none  [the longest x4 20.3 us: shards(): jnp.einsum('pij,pjk->pik', gram, basis, precision=lax.Precision.HIGHEST)]
    convert_element_type x1 -> x4, other arithmetic: 2.04 us -> 30.1 us  [shards(): theta.append(total.astype(jnp.bfloat16))]
  transfers between devices with their start and end apart: 4 -> 4, of which waited for: 4 -> 4; matrix products, arithmetic and copies ran while one was open for 0% -> 1% of each run, Pallas kernels for 0% -> 0%
where the time goes in v1:
time: 174 us; the launch traced here: 173 us
  waiting for transfers between devices  80.5 us (46%)
  Pallas kernels  43.6 us (25%)
  other arithmetic  30.4 us (17%)
  starting transfers between devices  12.1 us (7%)
  local copies, waits for them, and re-layouts  3.25 us (2%)
  matrix products  2.6 us (1%)
    ppermute x2, waiting for transfers between devices, from_behind(): lax.ppermute(value, axis, [(source, source + steps) for source in range(i...  44.9 us
    pallas_call x1, Pallas kernels, subspace(): pl.pallas_call(body, out_shape=(jax.ShapeDtypeStruct((S, d, n), BF), jax....  43.6 us
    ppermute x2, waiting for transfers between devices, shifted(): lax.ppermute(value, axis, [(i, (i + by) % peers) for i in range(peers)])  35.6 us
    convert_element_type x4, other arithmetic, shards(): theta.append(total.astype(jnp.bfloat16))  30.1 us
    ppermute x2, starting transfers between devices, from_behind(): lax.ppermute(value, axis, [(source, source + steps) for source in range(i...  6.76 us
    ppermute x2, starting transfers between devices, shifted(): lax.ppermute(value, axis, [(i, (i + by) % peers) for i in range(peers)])  5.31 us
  transfers between devices with their start and end apart: 4, of which 4 were waited for; matrix products, arithmetic and copies ran while one was open for 1% of the time, Pallas kernels for 0%

profile of v1, /device:TPU:24, one launch (start us, length us, event | category | flops | bytes accessed | tf_op | source)
XLA Modules:
  0.0 173.2 jit_solution(2812571643536670188)
XLA Ops:
  0.6 0.0 copy-start
  0.6 0.0 copy-start.4
  0.7 0.0 copy-start.3
  0.7 5.3 %collective-permute-start = (bf16[1,4,512,512]{3,2,1,0:T(8,128)(2,1)}, bf16[1,4,512,512]{3,2,1,0:T(8,128)(2,1)S(1)}, u32[]{:S(2)}, u32[]{:S(2)}) collective-permute-start(bf16[1,4,512,512]{3,2,1,0:T(8,128)(2,1)} %param.7), channel_id=1, source_target_pairs={{0,240},{16,0},{32,16},{48,32},{64,48},{80,64},{96,80},{112,96},{1... | collective-permute-start | bytes 6291464 | tf_op jit(solution)/shard_map/ppermute | solution.py:104
  6.0 23.9 %collective-permute-done = bf16[1,4,512,512]{3,2,1,0:T(8,128)(2,1)S(1)} collective-permute-done((bf16[1,4,512,512]{3,2,1,0:T(8,128)(2,1)}, bf16[1,4,512,512]{3,2,1,0:T(8,128)(2,1)S(1)}, u32[]{:S(2)}, u32[]{:S(2)}) %collective-permute-start) | collective-permute-done | bytes 2097184 | tf_op jit(solution)/shard_map/ppermute | solution.py:104
  29.8 0.0 copy-done
  29.8 2.6 %fusion.3 = bf16[4,512,512]{2,1,0:T(8,128)(2,1)} fusion(bf16[1,4,512,512]{3,2,1,0:T(8,128)(2,1)S(1)} %collective-permute-done, bf16[1,4,512,512]{3,2,1,0:T(8,128)(2,1)S(1)} %copy-done), kind=kOutput, calls=%fused_computation.4 | convolution fusion | flops 1074790400 | bytes 6291456 | tf_op jit(solution)/shard_map/qij,qjk->qik/dot_general | solution.py:122
  32.4 4.8 %collective-permute-start.2 = (bf16[4,512,512]{2,1,0:T(8,128)(2,1)}, bf16[4,512,512]{2,1,0:T(8,128)(2,1)}, u32[]{:S(2)}, u32[]{:S(2)}) collective-permute-start(bf16[4,512,512]{2,1,0:T(8,128)(2,1)} %fusion.3), channel_id=1, source_target_pairs={{1,0},{2,1},{3,2},{4,3},{5,4},{6,5},{7,6},{8,7},{9,8},{10,9},{11,1... | collective-permute-start | bytes 6291464 | tf_op jit(solution)/shard_map/ppermute | solution.py:110
  37.3 1.9 %collective-permute-start.1 = (bf16[4,512,512]{2,1,0:T(8,128)(2,1)}, bf16[4,512,512]{2,1,0:T(8,128)(2,1)}, u32[]{:S(2)}, u32[]{:S(2)}) collective-permute-start(bf16[4,512,512]{2,1,0:T(8,128)(2,1)} %fusion.3), channel_id=1, source_target_pairs={{0,1},{1,2},{2,3},{3,4},{4,5},{5,6},{6,7},{7,8},{8,9},{9,10},{10,1... | collective-permute-start | bytes 6291464 | tf_op jit(solution)/shard_map/ppermute | solution.py:110
  39.2 0.0 copy-done.4
  39.2 0.0 copy-done.3
  39.3 0.1 pad_dynamic-slice_fusion
  39.4 0.7 fusion.39
  40.0 0.7 fusion.38
  40.8 38.7 %collective-permute-done.2 = bf16[4,512,512]{2,1,0:T(8,128)(2,1)} collective-permute-done((bf16[4,512,512]{2,1,0:T(8,128)(2,1)}, bf16[4,512,512]{2,1,0:T(8,128)(2,1)}, u32[]{:S(2)}, u32[]{:S(2)}) %collective-permute-start.2) | collective-permute-done | bytes 2097184 | tf_op jit(solution)/shard_map/ppermute | solution.py:110
  79.4 6.2 %collective-permute-done.1 = bf16[4,512,512]{2,1,0:T(8,128)(2,1)} collective-permute-done((bf16[4,512,512]{2,1,0:T(8,128)(2,1)}, bf16[4,512,512]{2,1,0:T(8,128)(2,1)}, u32[]{:S(2)}, u32[]{:S(2)}) %collective-permute-start.1) | collective-permute-done | bytes 2097184 | tf_op jit(solution)/shard_map/ppermute | solution.py:110
  85.7 6.2 %fusion.36 = bf16[1,512,512]{2,1,0:T(8,128)(2,1)S(1)} fusion(f32[]{:T(128)} %bitcast.31, f32[]{:T(128)} %bitcast.30, f32[]{:T(128)} %bitcast.29, f32[]{:T(128)} %bitcast.28, f32[]{:T(128)} %bitcast.27, f32[]{:T(128)} %bitcast.26, bf16[4,512,512]{2,1,0:T(8,128)(2,1)} %collective-permute-done.2, bf16[4,512,512]{2,1,0:T(8,128)(2,1)} %fusion.3, ...), kind=kLoop, calls=%fused_computation.63 | loop fusion | flops 4718592 | bytes 3670040 | tf_op jit(solution)/shard_map/convert_element_type | solution.py:134
  91.8 6.1 %fusion.13 = bf16[1,512,512]{2,1,0:T(8,128)(2,1)S(1)} fusion(f32[]{:T(128)} %bitcast.7, f32[]{:T(128)} %bitcast.6, f32[]{:T(128)} %bitcast.5, f32[]{:T(128)} %bitcast.4, f32[]{:T(128)} %bitcast.3, f32[]{:T(128)} %bitcast, bf16[4,512,512]{2,1,0:T(8,128)(2,1)} %collective-permute-done.2, bf16[4,512,512]{2,1,0:T(8,128)(2,1)} %fusion.3, ...), kind=kLoop, calls=%fused_computation.40 | loop fusion | flops 4718592 | bytes 3670040 | tf_op jit(solution)/shard_map/convert_element_type | solution.py:134
  97.9 8.9 %fusion.30 = bf16[1,512,512]{2,1,0:T(8,128)(2,1)S(1)} fusion(f32[]{:T(128)} %bitcast.25, f32[]{:T(128)} %bitcast.24, f32[]{:T(128)} %bitcast.23, f32[]{:T(128)} %bitcast.22, f32[]{:T(128)} %bitcast.21, f32[]{:T(128)} %bitcast.20, f32[]{:T(128)} %bitcast.19, f32[]{:T(128)} %bitcast.18, f32[]{:T(128)} %bitcast.17, ...), kind=kLoop, calls=%fused_computation.57 | loop fusion | flops 7077888 | bytes 5242916 | tf_op jit(solution)/shard_map/convert_element_type | solution.py:134
  106.8 9.0 %fusion.22 = bf16[1,512,512]{2,1,0:T(8,128)(2,1)S(1)} fusion(f32[]{:T(128)} %bitcast.16, f32[]{:T(128)} %bitcast.15, f32[]{:T(128)} %bitcast.14, f32[]{:T(128)} %bitcast.13, f32[]{:T(128)} %bitcast.12, f32[]{:T(128)} %bitcast.11, f32[]{:T(128)} %bitcast.10, f32[]{:T(128)} %bitcast.9, f32[]{:T(128)} %bitcast.8, ...), kind=kLoop, calls=%fused_computation.49 | loop fusion | flops 7077888 | bytes 5242916 | tf_op jit(solution)/shard_map/convert_element_type | solution.py:134
  115.8 0.0 copy-start.1
  115.8 0.0 copy-start.2
  115.8 0.3 pad_maximum_fusion.theta
  116.1 0.9 copy-done.1
  117.0 0.0 copy-done.2
  117.0 43.6 %shard_map.77 = (bf16[4,512,128]{2,1,0:T(8,128)(2,1)}, bf16[4,128,512]{2,1,0:T(8,128)(2,1)S(1)}) custom-call(bf16[4,512,512]{2,1,0:T(8,128)(2,1)S(1)} %pad_maximum_fusion.theta, f32[4,512,128]{2,1,0:T(8,128)S(1)} %bitcast.43, s32[1,4]{1,0:T(1,128)S(1)} %copy-done.2), custom_call_target="tpu_custom_call" | custom-call | tf_op jit(solution)/shard_map/pallas_call | solution.py:93
  160.6 0.0 collective-permute-start.3
  160.6 11.8 %collective-permute-done.3 = bf16[1,4,128,512]{3,2,1,0:T(8,128)(2,1)S(1)} collective-permute-done((bf16[1,4,128,512]{3,2,1,0:T(8,128)(2,1)S(1)}, bf16[1,4,128,512]{3,2,1,0:T(8,128)(2,1)S(1)}, u32[]{:S(2)}, u32[]{:S(2)}) %collective-permute-start.3) | collective-permute-done | bytes 524320 | tf_op jit(solution)/shard_map/ppermute | solution.py:104
  172.4 0.8 copy.9
  (1 shorter events, 0.0 us)
Async XLA Ops:
  0.6 29.2 %copy-start = (bf16[1,4,512,512]{3,2,1,0:T(8,128)(2,1)S(1)}, bf16[1,4,512,512]{3,2,1,0:T(8,128)(2,1)}, u32[]{:S(2)}) copy-start(bf16[1,4,512,512]{3,2,1,0:T(8,128)(2,1)} %param.6) | copy-start | bytes 6291460
  0.6 38.6 %copy-start.4 = (s32[64,64]{1,0:T(8,128)S(1)}, s32[64,64]{1,0:T(8,128)}, u32[]{:S(2)}) copy-start(s32[64,64]{1,0:T(8,128)} %param.9) | copy-start | bytes 49156
  0.7 38.6 %copy-start.3 = (f32[64,64]{1,0:T(8,128)S(1)}, f32[64,64]{1,0:T(8,128)}, u32[]{:S(2)}) copy-start(f32[64,64]{1,0:T(8,128)} %param.8) | copy-start | bytes 49156
  0.7 29.2 %collective-permute-start = (bf16[1,4,512,512]{3,2,1,0:T(8,128)(2,1)}, bf16[1,4,512,512]{3,2,1,0:T(8,128)(2,1)S(1)}, u32[]{:S(2)}, u32[]{:S(2)}) collective-permute-start(bf16[1,4,512,512]{3,2,1,0:T(8,128)(2,1)} %param.7), channel_id=1, source_target_pairs={{0,240},{16,0},{32,16},{48,32},{64,48},{80,64},{96,80},{112,96},{1... | collective-permute-start | bytes 6291464 | tf_op jit(solution)/shard_map/ppermute | solution.py:104
  32.4 47.0 %collective-permute-start.2 = (bf16[4,512,512]{2,1,0:T(8,128)(2,1)}, bf16[4,512,512]{2,1,0:T(8,128)(2,1)}, u32[]{:S(2)}, u32[]{:S(2)}) collective-permute-start(bf16[4,512,512]{2,1,0:T(8,128)(2,1)} %fusion.3), channel_id=1, source_target_pairs={{1,0},{2,1},{3,2},{4,3},{5,4},{6,5},{7,6},{8,7},{9,8},{10,9},{11,1... | collective-permute-start | bytes 6291464 | tf_op jit(solution)/shard_map/ppermute | solution.py:110
  37.3 48.4 %collective-permute-start.1 = (bf16[4,512,512]{2,1,0:T(8,128)(2,1)}, bf16[4,512,512]{2,1,0:T(8,128)(2,1)}, u32[]{:S(2)}, u32[]{:S(2)}) collective-permute-start(bf16[4,512,512]{2,1,0:T(8,128)(2,1)} %fusion.3), channel_id=1, source_target_pairs={{0,1},{1,2},{2,3},{3,4},{4,5},{5,6},{6,7},{7,8},{8,9},{9,10},{10,1... | collective-permute-start | bytes 6291464 | tf_op jit(solution)/shard_map/ppermute | solution.py:110
  115.8 1.2 copy-start.1
  115.8 1.2 copy-start.2
  160.6 11.8 %collective-permute-start.3 = (bf16[1,4,128,512]{3,2,1,0:T(8,128)(2,1)S(1)}, bf16[1,4,128,512]{3,2,1,0:T(8,128)(2,1)S(1)}, u32[]{:S(2)}, u32[]{:S(2)}) collective-permute-start(bf16[1,4,128,512]{3,2,1,0:T(8,128)(2,1)S(1)} %bitcast.44), channel_id=1, source_target_pairs={{0,16},{16,32},{32,48},{48,64},{64,80},{80,96},{96,112},{112,128},... | collective-permute-start | bytes 1572872 | tf_op jit(solution)/shard_map/ppermute | solution.py:104

commit v2 on v1

v2 whole, which is shorter than its diff:
```python
import functools
import jax
import jax.numpy as jnp
from jax import lax
from jax.experimental import pallas as pl
from jax.experimental.pallas import tpu as pltpu
from jax.sharding import PartitionSpec as P

MESH = pl.DeviceIdType.MESH
ITERS=4
NB=16
F32=jnp.float32; BF=jnp.bfloat16

def split3(x):
    h=x.astype(BF)
    r=x-h.astype(F32)
    m=r.astype(BF)
    l=(r-m.astype(F32)).astype(BF)
    return h,m,l

def dot(a,b,ca,cb):
    return lax.dot_general(a,b,(((ca,),(cb,)),((),())),preferred_element_type=F32)

def dot6(a,b,ca,cb):
    ah,am,al=split3(a); bh,bm,bl=split3(b)
    return (dot(ah,bh,ca,cb)+(dot(ah,bm,ca,cb)+dot(am,bh,ca,cb))
            +(dot(ah,bl,ca,cb)+dot(am,bm,ca,cb)+dot(al,bh,ca,cb)))

def factor(aug, ubuf, tri, n, nb, S):
    for t in range(n//nb):
        lo=t*nb
        X=[aug[pl.ds(lo+k,2*S,stride=n),:] for k in range(nb)]
        v={}
        for i in range(nb):
            xa=jnp.concatenate([X[i][:S],X[i][:S]],axis=0)
            for k in range(i+1):
                v[i,k]=jnp.broadcast_to(xa[:,lo+k:lo+k+1],(2*S,n))
        U=[None]*nb
        for j in range(nb):
            r=lax.rsqrt(v[j,j])
            U[j]=X[j]*r
            tri[pl.ds(lo+j,S,stride=n),:]=U[j][S:]
            ubuf[pl.ds(j,2*S,stride=nb),:]=U[j]
            col={}
            for i in range(j+1,nb):
                col[i]=v[i,j]*r
            for i in range(j+1,nb):
                for k in range(j+1,i+1):
                    v[i,k]=v[i,k]-col[i]*col[k]
                X[i]=X[i]-col[i]*U[j]
        if lo+nb<n:
            for s in range(S):
                h,m,l=split3(ubuf[s*nb:(s+1)*nb,:])
                lhs=jnp.concatenate([h,h,m,h,m,l],axis=0)
                rhs=jnp.concatenate([h,m,h,l,m,h],axis=0)
                h,m,l=split3(ubuf[(S+s)*nb:(S+s+1)*nb,:])
                rhs2=jnp.concatenate([h,m,h,l,m,h],axis=0)
                up=dot(lhs,jnp.concatenate([rhs,rhs2],axis=1),0,0)
                rows=slice(s*n+lo+nb,(s+1)*n)
                aug[rows,:]=aug[rows,:]-up[lo+nb:,:n]
                rows=slice((S+s)*n+lo+nb,(S+s+1)*n)
                aug[rows,:]=aug[rows,:]-up[lo+nb:,n:]


def exchange_body(left, right, gate, sign, theta, left_v, partner, pair, below, above,
                  lsem, rs_sem, rr_sem, ps_sem, pr_sem):
    S, d, _ = left_v.shape
    bond, bonds = lax.axis_index("bond"), lax.axis_size("bond")
    f, nf = lax.axis_index("sec"), lax.axis_size("sec")
    ahead, behind = lax.rem(bond + 1, bonds), lax.rem(bond + bonds - 1, bonds)
    has_lo, has_hi = f > 0, f < nf - 1

    def load(q):
        return pltpu.make_async_copy(left.at[q], left_v.at[q], lsem.at[q])

    def shift(q):
        return pltpu.make_async_remote_copy(
            src_ref=right.at[q], dst_ref=partner.at[q], send_sem=rs_sem.at[q],
            recv_sem=rr_sem.at[q], device_id={"bond": behind}, device_id_type=MESH)

    def up(q):
        return pltpu.make_async_remote_copy(
            src_ref=pair.at[q], dst_ref=below.at[q], send_sem=ps_sem.at[0, q],
            recv_sem=pr_sem.at[0, q], device_id={"sec": f + 1}, device_id_type=MESH)

    def down(q):
        return pltpu.make_async_remote_copy(
            src_ref=pair.at[q], dst_ref=above.at[q], send_sem=ps_sem.at[1, q],
            recv_sem=pr_sem.at[1, q], device_id={"sec": f - 1}, device_id_type=MESH)

    for q in range(S):
        load(q).start()
    barrier = pltpu.get_barrier_semaphore()
    pl.semaphore_signal(barrier, inc=1, device_id={"bond": ahead}, device_id_type=MESH)
    pl.semaphore_signal(barrier, inc=1, device_id={"bond": behind}, device_id_type=MESH)

    @pl.when(has_lo)
    def _():
        pl.semaphore_signal(barrier, inc=1, device_id={"sec": f - 1}, device_id_type=MESH)

    @pl.when(has_hi)
    def _():
        pl.semaphore_signal(barrier, inc=1, device_id={"sec": f + 1}, device_id_type=MESH)

    pl.semaphore_wait(barrier, 2 + has_lo.astype(jnp.int32) + has_hi.astype(jnp.int32))

    for q in range(S):
        shift(q).start()

    @pl.when(jnp.logical_not(has_lo))
    def _():
        below[...] = jnp.zeros_like(below)

    @pl.when(jnp.logical_not(has_hi))
    def _():
        above[...] = jnp.zeros_like(above)

    def multiply(q, c):
        load(q).wait()
        shift(q).wait_recv()

        def rows(i, c):
            at = pl.ds(pl.multiple_of(i * 128, 128), 128)
            pair[q, at, :] = dot(left_v[q, at, :], partner[q], 1, 0).astype(BF)
            return c

        lax.fori_loop(0, d // 128, rows, 0)

        @pl.when(has_hi)
        def _():
            up(q).start()

        @pl.when(has_lo)
        def _():
            down(q).start()

        return c

    lax.fori_loop(0, S, multiply, 0)

    firsts = (jnp.maximum(f - 1, 0), f, jnp.minimum(f + 1, nf - 1))
    here = (has_lo.astype(F32), None, has_hi.astype(F32))

    def arrive(q):
        @pl.when(has_lo)
        def _():
            up(q).wait_recv()

        @pl.when(has_hi)
        def _():
            down(q).wait_recv()

    def mix(p):
        terms = []
        for first, gone, block in zip(firsts, here, (below, pair, above)):
            for q in range(max(0, p - 1), min(S, p + 2)):
                row, column = f * S + p, first * S + q
                w = gate[row, column] * (1.0 - 2.0 * sign[row, column].astype(F32))
                terms.append((w if gone is None else w * gone, block, q))

        def rows(i, c):
            at = pl.ds(pl.multiple_of(i * 16, 16), 16)
            total = None
            for w, block, q in terms:
                term = w * block[q, at, :].astype(F32)
                total = term if total is None else total + term
            theta[p, at, :] = total.astype(BF)
            return c

        lax.fori_loop(0, d // 16, rows, 0)

    arrive(0)
    arrive(1)
    mix(0)
    arrive(2)
    mix(1)
    arrive(3)
    mix(2)
    mix(3)
    for q in range(S):
        shift(q).wait_send()

        @pl.when(has_hi)
        def _():
            up(q).wait_send()

        @pl.when(has_lo)
        def _():
            down(q).wait_send()


def exchange(left, right, gate, sign):
    S, d, _ = left.shape
    block = pltpu.VMEM((S, d, d), BF)
    dma = pltpu.SemaphoreType.DMA
    hbm = pl.BlockSpec(memory_space=pl.ANY)
    smem = pl.BlockSpec(memory_space=pltpu.SMEM)
    return pl.pallas_call(
        exchange_body,
        out_shape=jax.ShapeDtypeStruct((S, d, d), BF),
        in_specs=[hbm, hbm, smem, smem],
        out_specs=pl.BlockSpec(memory_space=pltpu.VMEM),
        scratch_shapes=[block] * 5 + [dma((S,)), dma((S,)), dma((S,)), dma((2, S)), dma((2, S))],
        compiler_params=pltpu.CompilerParams(
            collective_id=0, has_side_effects=True, vmem_limit_bytes=24 * 2**20),
    )(left, right, gate, sign)


def iterate_body(theta, start, bt, gt, aug, ubuf, tri):
    S, d, n = start.shape
    eye = (lax.broadcasted_iota(jnp.int32, (n, n), 0)
           == lax.broadcasted_iota(jnp.int32, (n, n), 1)).astype(F32)
    for s in range(S):
        bt[s] = start[s].T

    def step(_, c):
        for s in range(S):
            th = theta[s]
            h, m, l = split3(bt[s])
            z = dot(h, th, 1, 0) + (dot(m, th, 1, 0) + dot(l, th, 1, 0))
            h, m, l = split3(z)
            g = dot(h, th, 1, 1) + (dot(m, th, 1, 1) + dot(l, th, 1, 1))
            gt[s] = g
            aug[s * n:(s + 1) * n, :] = dot6(g, g, 1, 1)
            aug[(S + s) * n:(S + s + 1) * n, :] = eye
        factor(aug, ubuf, tri, n, NB, S)
        for s in range(S):
            bt[s] = dot6(tri[s * n:(s + 1) * n, :], gt[s], 1, 0)
        return c

    lax.fori_loop(0, ITERS, step, 0)


def iterate(theta, start):
    S, d, n = start.shape
    vmem = pl.BlockSpec(memory_space=pltpu.VMEM)
    return pl.pallas_call(
        iterate_body,
        out_shape=jax.ShapeDtypeStruct((S, n, d), F32),
        in_specs=[vmem, vmem],
        out_specs=vmem,
        scratch_shapes=[
            pltpu.VMEM((S, n, d), F32),
            pltpu.VMEM((2 * S * n, n), F32),
            pltpu.VMEM((2 * S * NB, n), F32),
            pltpu.VMEM((S * n, n), F32),
        ],
        compiler_params=pltpu.CompilerParams(vmem_limit_bytes=24 * 2**20),
    )(theta, start)


def finish_body(theta, bt, kept, left_new, right_new, out, s_sem, r_sem):
    S, n, d = bt.shape
    bond, bonds = lax.axis_index("bond"), lax.axis_size("bond")
    ahead, behind = lax.rem(bond + 1, bonds), lax.rem(bond + bonds - 1, bonds)
    barrier = pltpu.get_barrier_semaphore()
    pl.semaphore_signal(barrier, inc=1, device_id={"bond": ahead}, device_id_type=MESH)
    pl.semaphore_signal(barrier, inc=1, device_id={"bond": behind}, device_id_type=MESH)
    row = lax.broadcasted_iota(jnp.int32, (n, d), 0)

    def back(s):
        return pltpu.make_async_remote_copy(
            src_ref=out.at[s], dst_ref=right_new.at[s], send_sem=s_sem.at[s],
            recv_sem=r_sem.at[s], device_id={"bond": ahead}, device_id_type=MESH)

    for s in range(S):
        masked = jnp.where(row < kept[0, s], bt[s], 0.0)
        h, m, l = split3(masked)
        th = theta[s]
        out[s] = (dot(h, th, 1, 0) + (dot(m, th, 1, 0) + dot(l, th, 1, 0))).astype(BF)
        if s == 0:
            pl.semaphore_wait(barrier, 2)
        back(s).start()
    for s in range(S):
        masked = jnp.where(row < kept[0, s], bt[s], 0.0)
        left_new[s] = masked.T.astype(BF)
    for s in range(S):
        back(s).wait()


def finish(theta, bt, kept):
    S, n, d = bt.shape
    vmem = pl.BlockSpec(memory_space=pltpu.VMEM)
    dma = pltpu.SemaphoreType.DMA
    return pl.pallas_call(
        finish_body,
        out_shape=(jax.ShapeDtypeStruct((S, d, n), BF), jax.ShapeDtypeStruct((S, n, d), BF)),
        in_specs=[vmem, vmem, pl.BlockSpec(memory_space=pltpu.SMEM)],
        out_specs=[vmem, pl.BlockSpec(memory_space=pl.ANY)],
        scratch_shapes=[pltpu.VMEM((S, n, d), BF), dma((S,)), dma((S,))],
        compiler_params=pltpu.CompilerParams(
            collective_id=1, has_side_effects=True, vmem_limit_bytes=24 * 2**20),
    )(theta, bt, kept)


def shards(left_site, right_site, gate, sign_table, kept, start):
    theta = exchange(left_site[0], right_site[0], gate, sign_table)
    bt = iterate(theta, start[0])
    left_new, right_new = finish(theta, bt, kept)
    return left_new[None], right_new[None]


def solution(mesh):
    return jax.shard_map(
        shards,
        mesh=mesh,
        in_specs=(
            P("bond", "sec", None, None),
            P("bond", "sec", None, None),
            P(),
            P(),
            P("bond", "sec"),
            P("bond", "sec", None, None),
        ),
        out_specs=(P("bond", "sec", None, None), P("bond", "sec", None, None)),
        check_vma=False,
    )
```

time: 174 us -> 118 us (0.68)
  waiting for transfers between devices: 80.5 us -> 0 us
  Pallas kernels: 43.6 us -> 111 us
  other arithmetic: 30.4 us -> 0 us
  starting transfers between devices: 12.1 us -> 0 us
  local copies, waits for them, and re-layouts: 3.25 us -> 6.29 us
  matrix products: 2.6 us -> 0 us
    ppermute x4 -> x0, waiting for transfers between devices: 80.5 us -> none  [the longest x2 44.9 us: from_behind(): lax.ppermute(value, axis, [(source, source + steps) for source in range(i...]
    pallas_call x1 -> x3, Pallas kernels: 43.6 us -> 111 us  [the longest x1 55.2 us: exchange(): pl.pallas_call(exchange_body, out_shape=jax.ShapeDtypeStruct((S, d, d), B...]
    convert_element_type x4 -> x0, other arithmetic: 30.1 us -> none  [shards(): theta.append(total.astype(jnp.bfloat16))]
    ppermute x4 -> x0, starting transfers between devices: 12.1 us -> none  [the longest x2 6.76 us: from_behind(): lax.ppermute(value, axis, [(source, source + steps) for source in range(i...]
    unnamed x11 -> x14, local copies, waits for them, and re-layouts: 1.75 us -> 6.29 us
    dot_general x1 -> x0, matrix products: 2.6 us -> none  [shards(): jnp.einsum('qij,qjk->qik', left_site[0], partner[0], preferred_element_ty...]
  transfers between devices with their start and end apart: 4 -> 0, of which waited for: 4 -> 0; matrix products, arithmetic and copies ran while one was open for 1% -> 0% of each run, Pallas kernels for 0% -> 0%
where the time goes in v2:
time: 118 us
  Pallas kernels  111 us (94%)
  local copies, waits for them, and re-layouts  6.29 us (5%)
    pallas_call x1, Pallas kernels, exchange(): pl.pallas_call(exchange_body, out_shape=jax.ShapeDtypeStruct((S, d, d), B...  55.2 us
    pallas_call x1, Pallas kernels, iterate(): pl.pallas_call(iterate_body, out_shape=jax.ShapeDtypeStruct((S, n, d), F3...  41.1 us
    pallas_call x1, Pallas kernels, finish(): pl.pallas_call(finish_body, out_shape=(jax.ShapeDtypeStruct((S, d, n), BF...  14.6 us
    unnamed x14, local copies, waits for them, and re-layouts  6.29 us

profile of v2, /device:TPU:24, one launch (start us, length us, event | category | flops | bytes accessed | tf_op | source)
XLA Modules:
  0.0 117.9 jit_solution(11487642424294561854)
XLA Ops:
  0.6 0.0 copy-start
  0.6 1.6 %copy-done = bf16[1,4,512,512]{3,2,1,0:T(8,128)(2,1)S(1)} copy-done((bf16[1,4,512,512]{3,2,1,0:T(8,128)(2,1)S(1)}, bf16[1,4,512,512]{3,2,1,0:T(8,128)(2,1)}, u32[]{:S(2)}) %copy-start) | copy-done | bytes 2097176
  2.2 0.0 copy-start.1
  2.2 1.6 %copy-done.1 = bf16[1,4,512,512]{3,2,1,0:T(8,128)(2,1)S(1)} copy-done((bf16[1,4,512,512]{3,2,1,0:T(8,128)(2,1)S(1)}, bf16[1,4,512,512]{3,2,1,0:T(8,128)(2,1)}, u32[]{:S(2)}) %copy-start.1) | copy-done | bytes 2097176
  3.8 0.0 copy-start.3
  3.8 0.8 copy-done.3
  4.6 0.0 copy-start.4
  4.6 0.8 copy-done.4
  5.3 0.0 copy-start.2
  5.3 55.2 %shard_map.77.theta = bf16[4,512,512]{2,1,0:T(8,128)(2,1)S(1)} custom-call(bf16[4,512,512]{2,1,0:T(8,128)(2,1)S(1)} %bitcast.5, bf16[4,512,512]{2,1,0:T(8,128)(2,1)S(1)} %bitcast.6, f32[64,64]{1,0:T(8,128)S(1)} %copy-done.3, s32[64,64]{1,0:T(8,128)S(1)} %copy-done.4), custom_call_target="tpu_custom_call" | custom-call | tf_op jit(solution)/shard_map/pallas_call | solution.py:198
  60.5 0.0 copy-done.2
  60.5 0.0 copy-start.5
  60.5 41.1 %shard_map.78.bt = f32[4,128,512]{2,1,0:T(8,128)S(1)} custom-call(bf16[4,512,512]{2,1,0:T(8,128)(2,1)S(1)} %shard_map.77.theta, f32[4,512,128]{2,1,0:T(8,128)S(1)} %bitcast.7), custom_call_target="tpu_custom_call" | custom-call | tf_op jit(solution)/shard_map/pallas_call | solution.py:237
  101.7 0.0 copy-done.5
  101.7 14.6 %shard_map.79 = (bf16[4,512,128]{2,1,0:T(8,128)(2,1)S(1)}, bf16[4,128,512]{2,1,0:T(8,128)(2,1)S(1)}) custom-call(bf16[4,512,512]{2,1,0:T(8,128)(2,1)S(1)} %shard_map.77.theta, f32[4,128,512]{2,1,0:T(8,128)S(1)} %shard_map.78.bt, s32[1,4]{1,0:T(1,128)S(1)} %copy-done.5), custom_call_target="tpu_custom_call" | custom-call | tf_op jit(solution)/shard_map/pallas_call | solution.py:285
  116.3 0.8 copy.10
  117.1 0.8 copy.11
Async XLA Ops:
  0.6 1.6 %copy-start = (bf16[1,4,512,512]{3,2,1,0:T(8,128)(2,1)S(1)}, bf16[1,4,512,512]{3,2,1,0:T(8,128)(2,1)}, u32[]{:S(2)}) copy-start(bf16[1,4,512,512]{3,2,1,0:T(8,128)(2,1)} %param.6) | copy-start | bytes 6291460
  2.2 1.6 %copy-start.1 = (bf16[1,4,512,512]{3,2,1,0:T(8,128)(2,1)S(1)}, bf16[1,4,512,512]{3,2,1,0:T(8,128)(2,1)}, u32[]{:S(2)}) copy-start(bf16[1,4,512,512]{3,2,1,0:T(8,128)(2,1)} %param.7) | copy-start | bytes 6291460
  3.8 0.8 copy-start.3
  4.6 0.8 copy-start.4
  5.3 55.2 %copy-start.2 = (f32[1,4,512,128]{3,2,1,0:T(8,128)S(1)}, f32[1,4,512,128]{3,2,1,0:T(8,128)}, u32[]{:S(2)}) copy-start(f32[1,4,512,128]{3,2,1,0:T(8,128)} %param.11) | copy-start | bytes 3145732
  60.5 41.2 %copy-start.5 = (s32[1,4]{1,0:T(1,128)S(1)}, s32[1,4]{1,0:T(1,128)}, u32[]{:S(2)}) copy-start(s32[1,4]{1,0:T(1,128)} %kept.1) | copy-start | bytes 52

commit v3 on v2

v3 whole, which is shorter than its diff:
```python
import functools
import jax
import jax.numpy as jnp
from jax import lax
from jax.experimental import pallas as pl
from jax.experimental.pallas import tpu as pltpu
from jax.sharding import PartitionSpec as P

MESH = pl.DeviceIdType.MESH
ITERS=4
NB=16
F32=jnp.float32; BF=jnp.bfloat16

def split3(x):
    h=x.astype(BF)
    r=x-h.astype(F32)
    m=r.astype(BF)
    l=(r-m.astype(F32)).astype(BF)
    return h,m,l

def split2(x):
    h = x.astype(BF)
    return h, (x - h.astype(F32)).astype(BF)


def dot(a,b,ca,cb):
    return lax.dot_general(a,b,(((ca,),(cb,)),((),())),preferred_element_type=F32)

def factor(aug, ubuf, tri, n, nb, S):
    for t in range(n//nb):
        lo=t*nb
        X=[aug[pl.ds(lo+k,2*S,stride=n),:] for k in range(nb)]
        v={}
        for i in range(nb):
            xa=jnp.concatenate([X[i][:S],X[i][:S]],axis=0)
            for k in range(i+1):
                v[i,k]=jnp.broadcast_to(xa[:,lo+k:lo+k+1],(2*S,n))
        U=[None]*nb
        for j in range(nb):
            r=lax.rsqrt(v[j,j])
            U[j]=X[j]*r
            tri[pl.ds(lo+j,S,stride=n),:]=U[j][S:]
            ubuf[pl.ds(j,2*S,stride=nb),:]=U[j]
            col={}
            for i in range(j+1,nb):
                col[i]=v[i,j]*r
            for i in range(j+1,nb):
                for k in range(j+1,i+1):
                    v[i,k]=v[i,k]-col[i]*col[k]
                X[i]=X[i]-col[i]*U[j]
        if lo+nb<n:
            for s in range(S):
                h,m,l=split3(ubuf[s*nb:(s+1)*nb,:])
                lhs=jnp.concatenate([h,h,m,h,m,l],axis=0)
                rhs=jnp.concatenate([h,m,h,l,m,h],axis=0)
                h,m,l=split3(ubuf[(S+s)*nb:(S+s+1)*nb,:])
                rhs2=jnp.concatenate([h,m,h,l,m,h],axis=0)
                up=dot(lhs,jnp.concatenate([rhs,rhs2],axis=1),0,0)
                rows=slice(s*n+lo+nb,(s+1)*n)
                aug[rows,:]=aug[rows,:]-up[lo+nb:,:n]
                rows=slice((S+s)*n+lo+nb,(S+s+1)*n)
                aug[rows,:]=aug[rows,:]-up[lo+nb:,n:]


def sum_rows(x, n):
    total = x[:n]
    for i in range(1, x.shape[0] // n):
        total = total + x[i * n:(i + 1) * n]
    return total


def layer_body(left, right, gate, sign, kept, start, left_new, right_new,
               left_v, partner, pair, below, above, theta, gram, start_v, gate_v, sign_v,
               bt, gt, aug, ubuf, tri, out,
               lsem, rs_sem, rr_sem, ps_sem, pr_sem, os_sem, or_sem):
    S, d, _ = left_v.shape
    n = bt.shape[1]
    bond, bonds = lax.axis_index("bond"), lax.axis_size("bond")
    f, nf = lax.axis_index("sec"), lax.axis_size("sec")
    ahead, behind = lax.rem(bond + 1, bonds), lax.rem(bond + bonds - 1, bonds)
    has_lo, has_hi = f > 0, f < nf - 1

    def load(q):
        return pltpu.make_async_copy(left.at[q], left_v.at[q], lsem.at[q])

    small = [
        pltpu.make_async_copy(start, start_v, lsem.at[S]),
        pltpu.make_async_copy(gate, gate_v, lsem.at[S + 1]),
        pltpu.make_async_copy(sign, sign_v, lsem.at[S + 2]),
    ]

    def shift(q):
        return pltpu.make_async_remote_copy(
            src_ref=right.at[q], dst_ref=partner.at[q], send_sem=rs_sem.at[q],
            recv_sem=rr_sem.at[q], device_id={"bond": behind}, device_id_type=MESH)

    def up(q):
        return pltpu.make_async_remote_copy(
            src_ref=pair.at[q], dst_ref=below.at[q], send_sem=ps_sem.at[0, q],
            recv_sem=pr_sem.at[0, q], device_id={"sec": f + 1}, device_id_type=MESH)

    def down(q):
        return pltpu.make_async_remote_copy(
            src_ref=pair.at[q], dst_ref=above.at[q], send_sem=ps_sem.at[1, q],
            recv_sem=pr_sem.at[1, q], device_id={"sec": f - 1}, device_id_type=MESH)

    def back(s):
        return pltpu.make_async_remote_copy(
            src_ref=out.at[s], dst_ref=right_new.at[s], send_sem=os_sem.at[s],
            recv_sem=or_sem.at[s], device_id={"bond": ahead}, device_id_type=MESH)

    barrier = pltpu.get_barrier_semaphore()
    pl.semaphore_signal(barrier, inc=1, device_id={"bond": ahead}, device_id_type=MESH)
    pl.semaphore_signal(barrier, inc=1, device_id={"bond": behind}, device_id_type=MESH)

    @pl.when(has_lo)
    def _():
        pl.semaphore_signal(barrier, inc=1, device_id={"sec": f - 1}, device_id_type=MESH)

    @pl.when(has_hi)
    def _():
        pl.semaphore_signal(barrier, inc=1, device_id={"sec": f + 1}, device_id_type=MESH)

    for q in range(S):
        load(q).start()
    for copy in small:
        copy.start()
    pl.semaphore_wait(barrier, 2 + has_lo.astype(jnp.int32) + has_hi.astype(jnp.int32))
    for q in range(S):
        shift(q).start()

    @pl.when(jnp.logical_not(has_lo))
    def _():
        below[...] = jnp.zeros_like(below)

    @pl.when(jnp.logical_not(has_hi))
    def _():
        above[...] = jnp.zeros_like(above)

    def multiply(q, c):
        load(q).wait()
        shift(q).wait_recv()

        def rows(i, c):
            at = pl.ds(pl.multiple_of(i * 128, 128), 128)
            pair[q, at, :] = dot(left_v[q, at, :], partner[q], 1, 0).astype(BF)
            return c

        lax.fori_loop(0, d // 128, rows, 0)

        @pl.when(has_hi)
        def _():
            up(q).start()

        @pl.when(has_lo)
        def _():
            down(q).start()

        return c

    lax.fori_loop(0, S, multiply, 0)
    for copy in small:
        copy.wait()

    firsts = (jnp.maximum(f - 1, 0), f, jnp.minimum(f + 1, nf - 1))
    here = (has_lo.astype(F32), None, has_hi.astype(F32))

    def arrive(q):
        @pl.when(has_lo)
        def _():
            up(q).wait_recv()

        @pl.when(has_hi)
        def _():
            down(q).wait_recv()

    def mix(p):
        terms = []
        for first, gone, block in zip(firsts, here, (below, pair, above)):
            for q in range(max(0, p - 1), min(S, p + 2)):
                row, column = f * S + p, first * S + q
                w = gate_v[row, column] * (1.0 - 2.0 * sign_v[row, column].astype(F32))
                terms.append((w if gone is None else w * gone, block, q))

        def rows(i, c):
            at = pl.ds(pl.multiple_of(i * 16, 16), 16)
            total = None
            for w, block, q in terms:
                term = w * block[q, at, :].astype(F32)
                total = term if total is None else total + term
            theta[p, at, :] = total.astype(BF)
            return c

        lax.fori_loop(0, d // 16, rows, 0)

    def grow(s, b):
        h, m = split2(b)
        g = (sum_rows(dot(jnp.concatenate([h, m], axis=0), gram[s, 0], 1, 0), n)
             + dot(h, gram[s, 1], 1, 0))
        gt[s] = g
        hm = jnp.concatenate(split2(g), axis=0)
        o = dot(hm, hm, 1, 1)
        aug[pl.ds(pl.multiple_of(s * n, n), n), :] = (o[:n, :n] + o[n:, n:]) + (o[:n, n:] + o[n:, :n])
        eye = (lax.broadcasted_iota(jnp.int32, (n, n), 0)
               == lax.broadcasted_iota(jnp.int32, (n, n), 1)).astype(F32)
        aug[pl.ds(pl.multiple_of((S + s) * n, n), n), :] = eye

    def begin(s, c):
        def rows(i, c):
            at = pl.ds(pl.multiple_of(i * 128, 128), 128)
            h, m = split2(dot(theta[s, at, :], theta[s], 1, 1))
            gram[s, 0, at, :] = h
            gram[s, 1, at, :] = m
            return c

        lax.fori_loop(0, d // 128, rows, 0)
        grow(s, start_v[s].T)
        return c

    arrive(0)
    arrive(1)
    mix(0)
    arrive(2)
    mix(1)
    arrive(3)
    mix(2)
    mix(3)
    lax.fori_loop(0, S, begin, 0)

    def step(it, c):
        factor(aug, ubuf, tri, n, NB, S)

        def normal(s, c):
            a, b, l = split3(tri[pl.ds(pl.multiple_of(s * n, n), n), :])
            lhs = jnp.concatenate([jnp.concatenate([x, x], axis=1) for x in (a, b, l)], axis=0)
            basis = sum_rows(dot(lhs, jnp.concatenate(split2(gt[s]), axis=0), 1, 0), n)

            @pl.when(it < ITERS - 1)
            def _():
                grow(s, basis)

            @pl.when(it == ITERS - 1)
            def _():
                bt[s] = basis

            return c

        lax.fori_loop(0, S, normal, 0)
        return c

    lax.fori_loop(0, ITERS, step, 0)
    row = lax.broadcasted_iota(jnp.int32, (n, d), 0)
    for s in range(S):
        masked = jnp.where(row < kept[0, s], bt[s], 0.0)
        out[s] = sum_rows(dot(jnp.concatenate(split2(masked), axis=0), theta[s], 1, 0), n).astype(BF)
        back(s).start()
    for s in range(S):
        left_new[s] = jnp.where(row < kept[0, s], bt[s], 0.0).T.astype(BF)
    for q in range(S):
        shift(q).wait_send()

        @pl.when(has_hi)
        def _():
            up(q).wait_send()

        @pl.when(has_lo)
        def _():
            down(q).wait_send()

    for s in range(S):
        back(s).wait()


def layer(left, right, gate, sign, kept, start):
    S, d, n = start.shape
    block = pltpu.VMEM((S, d, d), BF)
    dma = pltpu.SemaphoreType.DMA
    hbm = pl.BlockSpec(memory_space=pl.ANY)
    smem = pl.BlockSpec(memory_space=pltpu.SMEM)
    return pl.pallas_call(
        layer_body,
        out_shape=(jax.ShapeDtypeStruct((S, d, n), BF), jax.ShapeDtypeStruct((S, n, d), BF)),
        in_specs=[hbm, hbm, hbm, hbm, smem, hbm],
        out_specs=[pl.BlockSpec(memory_space=pltpu.VMEM), hbm],
        scratch_shapes=[block] * 6 + [
            pltpu.VMEM((S, 2, d, d), BF),
            pltpu.VMEM((S, d, n), F32),
            pltpu.SMEM(gate.shape, F32),
            pltpu.SMEM(sign.shape, jnp.int32),
            pltpu.VMEM((S, n, d), F32),
            pltpu.VMEM((S, n, d), F32),
            pltpu.VMEM((2 * S * n, n), F32),
            pltpu.VMEM((2 * S * NB, n), F32),
            pltpu.VMEM((S * n, n), F32),
            pltpu.VMEM((S, n, d), BF),
            dma((S + 3,)), dma((S,)), dma((S,)), dma((2, S)), dma((2, S)), dma((S,)), dma((S,)),
        ],
        compiler_params=pltpu.CompilerParams(
            collective_id=0, has_side_effects=True, vmem_limit_bytes=56 * 2**20),
    )(left, right, gate, sign, kept, start)


def shards(left_site, right_site, gate, sign_table, kept, start):
    left_new, right_new = layer(left_site[0], right_site[0], gate, sign_table, kept, start[0])
    return left_new[None], right_new[None]


def solution(mesh):
    return jax.shard_map(
        shards,
        mesh=mesh,
        in_specs=(
            P("bond", "sec", None, None),
            P("bond", "sec", None, None),
            P(),
            P(),
            P("bond", "sec"),
            P("bond", "sec", None, None),
        ),
        out_specs=(P("bond", "sec", None, None), P("bond", "sec", None, None)),
        check_vma=False,
    )
```

time: 118 us -> 113 us (0.958)
  local copies, waits for them, and re-layouts: 6.29 us -> 3.74 us
  Pallas kernels: 111 us -> 109 us
    unnamed x14 -> x2, local copies, waits for them, and re-layouts: 6.29 us -> 3.74 us
    pallas_call x3 -> x1, Pallas kernels: 111 us -> 109 us  [layer(): pl.pallas_call(layer_body, out_shape=(jax.ShapeDtypeStruct((S, d, n), BF)...]
where the time goes in v3:
time: 113 us
  Pallas kernels  109 us (96%)
  local copies, waits for them, and re-layouts  3.74 us (3%)
    pallas_call x1, Pallas kernels, layer(): pl.pallas_call(layer_body, out_shape=(jax.ShapeDtypeStruct((S, d, n), BF)...  109 us
    unnamed x2, local copies, waits for them, and re-layouts  3.74 us

profile of v3, /device:TPU:24, one launch (start us, length us, event | category | flops | bytes accessed | tf_op | source)
XLA Modules:
  0.0 113.1 jit_solution(1393544175314165706)
XLA Ops:
  0.6 108.8 %shard_map.77 = (bf16[4,512,128]{2,1,0:T(8,128)(2,1)}, bf16[4,128,512]{2,1,0:T(8,128)(2,1)}) custom-call(bf16[4,512,512]{2,1,0:T(8,128)(2,1)} %bitcast.5, bf16[4,512,512]{2,1,0:T(8,128)(2,1)} %bitcast.6, f32[64,64]{1,0:T(8,128)} %gate.1, s32[64,64]{1,0:T(8,128)} %sign.1, s32[1,4]{1,0:T(1,128)} %kept.1, f32[4,512,128]{2,1,0:T(8,128)} %bitcast.7), custom_call_target="tpu_custom_call" | custom-call | tf_op jit(solution)/shard_map/pallas_call | solution.py:280
  109.4 1.9 %copy.10 = bf16[1,4,512,128]{3,2,1,0:T(8,128)(2,1)} copy(bf16[1,4,512,128]{3,2,1,0:T(8,128)(2,1)} %bitcast.9) | data formatting | bytes 1048576
  111.3 1.9 %copy.11 = bf16[1,4,128,512]{3,2,1,0:T(8,128)(2,1)} copy(bf16[1,4,128,512]{3,2,1,0:T(8,128)(2,1)} %bitcast.8) | data formatting | bytes 1048576

commit v4 on v3

--- a/solution.py
+++ b/solution.py
@@ -26,41 +26,43 @@
 def dot(a,b,ca,cb):
     return lax.dot_general(a,b,(((ca,),(cb,)),((),())),preferred_element_type=F32)
 
-def factor(aug, ubuf, tri, n, nb, S):
+def factor(aug, ubuf, nbuf, tri, n, S, nb, hook):
+    lane=lax.broadcasted_iota(jnp.int32,(S,n),1)
+    lane1=lax.broadcasted_iota(jnp.int32,(1,n),1)
+    def bc(x,i): return jnp.broadcast_to(x[:,i:i+1],(S,n))
+    def within(a,b): return jnp.logical_and(lane>=a,lane<b)
+    X=[aug[pl.ds(k,S,stride=n),:] for k in range(nb)]
     for t in range(n//nb):
-        lo=t*nb
-        X=[aug[pl.ds(lo+k,2*S,stride=n),:] for k in range(nb)]
-        v={}
-        for i in range(nb):
-            xa=jnp.concatenate([X[i][:S],X[i][:S]],axis=0)
-            for k in range(i+1):
-                v[i,k]=jnp.broadcast_to(xa[:,lo+k:lo+k+1],(2*S,n))
-        U=[None]*nb
+        lo=t*nb; end=lo+nb
+        v={(i,k):bc(X[i],lo+k) for k in range(nb) for i in range(k,nb)}
         for j in range(nb):
             r=lax.rsqrt(v[j,j])
-            U[j]=X[j]*r
-            tri[pl.ds(lo+j,S,stride=n),:]=U[j][S:]
-            ubuf[pl.ds(j,2*S,stride=nb),:]=U[j]
-            col={}
-            for i in range(j+1,nb):
-                col[i]=v[i,j]*r
+            U=jnp.where(lane==lo+j,r,X[j]*r)
+            tri[pl.ds(lo+j,S,stride=n),:]=jnp.where(lane<=lo+j,U,0.0)
+            if end<n:
+                ubuf[pl.ds(j,S,stride=nb),:]=jnp.where(within(lo+j+1,end),0.0,U) if j<nb-1 else U
+            col={i:v[i,j]*r for i in range(j+1,nb)}
             for i in range(j+1,nb):
                 for k in range(j+1,i+1):
                     v[i,k]=v[i,k]-col[i]*col[k]
-                X[i]=X[i]-col[i]*U[j]
-        if lo+nb<n:
+                X[i]=jnp.where(lane==lo+j,0.0,X[i])-col[i]*U
+        if end<n:
+            blk=jnp.logical_and(lane1>=lo,lane1<end)
+            lt,rh=[],[]
             for s in range(S):
                 h,m,l=split3(ubuf[s*nb:(s+1)*nb,:])
-                lhs=jnp.concatenate([h,h,m,h,m,l],axis=0)
-                rhs=jnp.concatenate([h,m,h,l,m,h],axis=0)
-                h,m,l=split3(ubuf[(S+s)*nb:(S+s+1)*nb,:])
-                rhs2=jnp.concatenate([h,m,h,l,m,h],axis=0)
-                up=dot(lhs,jnp.concatenate([rhs,rhs2],axis=1),0,0)
-                rows=slice(s*n+lo+nb,(s+1)*n)
-                aug[rows,:]=aug[rows,:]-up[lo+nb:,:n]
-                rows=slice((S+s)*n+lo+nb,(S+s+1)*n)
-                aug[rows,:]=aug[rows,:]-up[lo+nb:,n:]
-
+                lt.append(jnp.concatenate([h,h,m,h,m,l],axis=0).T)
+                rh.append(jnp.concatenate([h,m,h,l,m,h],axis=0))
+            o=dot(jnp.concatenate([x[end:end+nb] for x in lt],axis=0),jnp.concatenate(rh,axis=1),1,0)
+            for s in range(S):
+                nbuf[s*nb:(s+1)*nb,:]=jnp.where(blk,0.0,aug[s*n+end:s*n+end+nb,:])-o[s*nb:(s+1)*nb,s*n:(s+1)*n]
+            X=[nbuf[pl.ds(k,S,stride=nb),:] for k in range(nb)]
+            first=end+nb
+            hook(t)
+            if first<n:
+                for s in range(S):
+                    rows=slice(s*n+first,(s+1)*n)
+                    aug[rows,:]=jnp.where(blk,0.0,aug[rows,:])-dot(lt[s][first:],rh[s],1,0)
 
 def sum_rows(x, n):
     total = x[:n]
@@ -71,14 +73,15 @@
 
 def layer_body(left, right, gate, sign, kept, start, left_new, right_new,
                left_v, partner, pair, below, above, theta, gram, start_v, gate_v, sign_v,
-               bt, gt, aug, ubuf, tri, out,
-               lsem, rs_sem, rr_sem, ps_sem, pr_sem, os_sem, or_sem):
+               bt, gt, ht, aug, ubuf, nbuf, tri, out,
+               lsem, rs_sem, rr_sem, ps_sem, pr_sem, os_sem, or_sem, turn):
     S, d, _ = left_v.shape
     n = bt.shape[1]
     bond, bonds = lax.axis_index("bond"), lax.axis_size("bond")
     f, nf = lax.axis_index("sec"), lax.axis_size("sec")
     ahead, behind = lax.rem(bond + 1, bonds), lax.rem(bond + bonds - 1, bonds)
     has_lo, has_hi = f > 0, f < nf - 1
+    even = lax.rem(bond, 2) == 0
 
     def load(q):
         return pltpu.make_async_copy(left.at[q], left_v.at[q], lsem.at[q])
@@ -148,6 +151,10 @@
 
         lax.fori_loop(0, d // 128, rows, 0)
 
+        @pl.when(jnp.logical_and(even, q == S - 1))
+        def _():
+            pl.semaphore_wait(turn, 1)
+
         @pl.when(has_hi)
         def _():
             up(q).start()
@@ -161,6 +168,22 @@
     lax.fori_loop(0, S, multiply, 0)
     for copy in small:
         copy.wait()
+    for s in range(S):
+        bt[s] = start_v[s].T
+
+    @pl.when(jnp.logical_not(even))
+    def _():
+        for q in range(S):
+            @pl.when(has_hi)
+            def _():
+                up(q).wait_send()
+
+            @pl.when(has_lo)
+            def _():
+                down(q).wait_send()
+
+        pl.semaphore_signal(turn, inc=1, device_id={"bond": behind}, device_id_type=MESH)
+
 
     firsts = (jnp.maximum(f - 1, 0), f, jnp.minimum(f + 1, nf - 1))
     here = (has_lo.astype(F32), None, has_hi.astype(F32))
@@ -193,19 +216,23 @@
 
         lax.fori_loop(0, d // 16, rows, 0)
 
-    def grow(s, b):
-        h, m = split2(b)
-        g = (sum_rows(dot(jnp.concatenate([h, m], axis=0), gram[s, 0], 1, 0), n)
-             + dot(h, gram[s, 1], 1, 0))
+    def by_gram(s, x):
+        h, m = split2(x)
+        return (sum_rows(dot(jnp.concatenate([h, m], axis=0), gram[s, 0], 1, 0), n)
+                + dot(h, gram[s, 1], 1, 0))
+
+    def by_tri(s, x):
+        a, b, l = split3(tri[s * n:(s + 1) * n, :])
+        lhs = jnp.concatenate([jnp.concatenate([y, y], axis=1) for y in (a, b, l)], axis=0)
+        return sum_rows(dot(lhs, jnp.concatenate(split2(x), axis=0), 1, 0), n)
+
+    def put(s, g):
         gt[s] = g
         hm = jnp.concatenate(split2(g), axis=0)
         o = dot(hm, hm, 1, 1)
-        aug[pl.ds(pl.multiple_of(s * n, n), n), :] = (o[:n, :n] + o[n:, n:]) + (o[:n, n:] + o[n:, :n])
-        eye = (lax.broadcasted_iota(jnp.int32, (n, n), 0)
-               == lax.broadcasted_iota(jnp.int32, (n, n), 1)).astype(F32)
-        aug[pl.ds(pl.multiple_of((S + s) * n, n), n), :] = eye
-
-    def begin(s, c):
+        aug[s * n:(s + 1) * n, :] = (o[:n, :n] + o[n:, n:]) + (o[:n, n:] + o[n:, :n])
+
+    def begin(s):
         def rows(i, c):
             at = pl.ds(pl.multiple_of(i * 128, 128), 128)
             h, m = split2(dot(theta[s, at, :], theta[s], 1, 1))
@@ -214,56 +241,52 @@
             return c
 
         lax.fori_loop(0, d // 128, rows, 0)
-        grow(s, start_v[s].T)
-        return c
+        put(s, by_gram(s, bt[s]))
 
     arrive(0)
     arrive(1)
     mix(0)
+    begin(0)
     arrive(2)
     mix(1)
+    begin(1)
     arrive(3)
     mix(2)
     mix(3)
-    lax.fori_loop(0, S, begin, 0)
+    begin(2)
+    begin(3)
 
     def step(it, c):
-        factor(aug, ubuf, tri, n, NB, S)
-
-        def normal(s, c):
-            a, b, l = split3(tri[pl.ds(pl.multiple_of(s * n, n), n), :])
-            lhs = jnp.concatenate([jnp.concatenate([x, x], axis=1) for x in (a, b, l)], axis=0)
-            basis = sum_rows(dot(lhs, jnp.concatenate(split2(gt[s]), axis=0), 1, 0), n)
-
-            @pl.when(it < ITERS - 1)
-            def _():
-                grow(s, basis)
-
-            @pl.when(it == ITERS - 1)
-            def _():
-                bt[s] = basis
-
-            return c
-
-        lax.fori_loop(0, S, normal, 0)
+        def meanwhile(t):
+            if t % 2 == 0 and t // 2 < S:
+                ht[t // 2] = by_gram(t // 2, gt[t // 2])
+
+        factor(aug, ubuf, nbuf, tri, n, S, NB, meanwhile)
+
+        @pl.when(it < ITERS - 1)
+        def _():
+            for s in range(S):
+                put(s, by_tri(s, ht[s]))
+
         return c
 
     lax.fori_loop(0, ITERS, step, 0)
     row = lax.broadcasted_iota(jnp.int32, (n, d), 0)
     for s in range(S):
-        masked = jnp.where(row < kept[0, s], bt[s], 0.0)
+        masked = jnp.where(row < kept[0, s], by_tri(s, gt[s]), 0.0)
+        bt[s] = masked
         out[s] = sum_rows(dot(jnp.concatenate(split2(masked), axis=0), theta[s], 1, 0), n).astype(BF)
         back(s).start()
     for s in range(S):
-        left_new[s] = jnp.where(row < kept[0, s], bt[s], 0.0).T.astype(BF)
+        left_new[s] = bt[s].T.astype(BF)
     for q in range(S):
         shift(q).wait_send()
 
-        @pl.when(has_hi)
+        @pl.when(jnp.logical_and(even, has_hi))
         def _():
             up(q).wait_send()
 
-        @pl.when(has_lo)
+        @pl.when(jnp.logical_and(even, has_lo))
         def _():
             down(q).wait_send()
 
@@ -275,13 +298,13 @@
     S, d, n = start.shape
     block = pltpu.VMEM((S, d, d), BF)
     dma = pltpu.SemaphoreType.DMA
-    hbm = pl.BlockSpec(memory_space=pl.ANY)
+    hbm = pl.BlockSpec(memory_space=pltpu.HBM)
     smem = pl.BlockSpec(memory_space=pltpu.SMEM)
     return pl.pallas_call(
         layer_body,
         out_shape=(jax.ShapeDtypeStruct((S, d, n), BF), jax.ShapeDtypeStruct((S, n, d), BF)),
         in_specs=[hbm, hbm, hbm, hbm, smem, hbm],
-        out_specs=[pl.BlockSpec(memory_space=pltpu.VMEM), hbm],
+        out_specs=[pl.BlockSpec(memory_space=pltpu.VMEM), pl.BlockSpec(memory_space=pl.ANY)],
         scratch_shapes=[block] * 6 + [
             pltpu.VMEM((S, 2, d, d), BF),
             pltpu.VMEM((S, d, n), F32),
@@ -289,14 +312,17 @@
             pltpu.SMEM(sign.shape, jnp.int32),
             pltpu.VMEM((S, n, d), F32),
             pltpu.VMEM((S, n, d), F32),
-            pltpu.VMEM((2 * S * n, n), F32),
-            pltpu.VMEM((2 * S * NB, n), F32),
+            pltpu.VMEM((S, n, d), F32),
+            pltpu.VMEM((S * n, n), F32),
+            pltpu.VMEM((S * NB, n), F32),
+            pltpu.VMEM((S * NB, n), F32),
             pltpu.VMEM((S * n, n), F32),
             pltpu.VMEM((S, n, d), BF),
             dma((S + 3,)), dma((S,)), dma((S,)), dma((2, S)), dma((2, S)), dma((S,)), dma((S,)),
+            pltpu.SemaphoreType.REGULAR,
         ],
         compiler_params=pltpu.CompilerParams(
-            collective_id=0, has_side_effects=True, vmem_limit_bytes=56 * 2**20),
+            collective_id=0, has_side_effects=True, vmem_limit_bytes=52 * 2**20),
     )(left, right, gate, sign, kept, start)
 
 

time: 113 us -> 98.7 us (0.87)
  Pallas kernels: 109 us -> 94.1 us
    pallas_call x1, Pallas kernels: 109 us -> 94.1 us  [layer(): pl.pallas_call(layer_body, out_shape=(jax.ShapeDtypeStruct((S, d, n), BF)...]
    unnamed x2 -> x8, local copies, waits for them, and re-layouts: 3.74 us -> 3.75 us
where the time goes in v4:
time: 98.7 us; the launch traced here: 98.5 us
  Pallas kernels  94.1 us (95%)
  local copies, waits for them, and re-layouts  3.75 us (4%)
    pallas_call x1, Pallas kernels, layer(): pl.pallas_call(layer_body, out_shape=(jax.ShapeDtypeStruct((S, d, n), BF)...  94.1 us
    unnamed x8, local copies, waits for them, and re-layouts  3.75 us

profile of v4, /device:TPU:24, one launch (start us, length us, event | category | flops | bytes accessed | tf_op | source)
XLA Modules:
  0.0 98.5 jit_solution(5891132134767386928)
XLA Ops:
  0.6 0.0 copy-start
  0.6 0.7 copy-done
  1.4 0.0 copy-start.1
  1.4 0.8 copy-done.1
  2.1 0.0 copy-start.2
  2.2 0.7 copy-done.2
  2.8 94.1 %shard_map.77 = (bf16[4,512,128]{2,1,0:T(8,128)(2,1)S(1)}, bf16[4,128,512]{2,1,0:T(8,128)(2,1)S(1)}) custom-call(bf16[4,512,512]{2,1,0:T(8,128)(2,1)} %bitcast.7, bf16[4,512,512]{2,1,0:T(8,128)(2,1)} %bitcast.8, f32[64,64]{1,0:T(8,128)S(1)} %copy-done, s32[64,64]{1,0:T(8,128)S(1)} %copy-done.1, s32[1,4]{1,0:T(1,128)S(1)} %copy-done.2, f32[4,512,128]{2,1,0:T(8,128)} %bitcast.9), custom_call_target="tpu_custom_call" | custom-call | tf_op jit(solution)/shard_map/pallas_call | solution.py:303
  96.9 0.8 copy.10
  97.7 0.8 copy.11
Async XLA Ops:
  0.6 0.8 copy-start
  1.4 0.8 copy-start.1
  2.1 0.7 copy-start.2

commit v5 on v4

--- a/solution.py
+++ b/solution.py
@@ -7,8 +7,8 @@
 from jax.sharding import PartitionSpec as P
 
 MESH = pl.DeviceIdType.MESH
-ITERS=4
-NB=16
+ITERS = 4
+NB = 16
 F32=jnp.float32; BF=jnp.bfloat16
 
 def split3(x):
@@ -71,8 +71,8 @@
     return total
 
 
-def layer_body(left, right, gate, sign, kept, start, left_new, right_new,
-               left_v, partner, pair, below, above, theta, gram, start_v, gate_v, sign_v,
+def layer_body(left, right, table, start, left_new, right_new,
+               left_v, partner, pair, below, above, theta, total, gram, start_v, table_v,
                bt, gt, ht, aug, ubuf, nbuf, tri, out,
                lsem, rs_sem, rr_sem, ps_sem, pr_sem, os_sem, or_sem, turn):
     S, d, _ = left_v.shape
@@ -81,36 +81,52 @@
     f, nf = lax.axis_index("sec"), lax.axis_size("sec")
     ahead, behind = lax.rem(bond + 1, bonds), lax.rem(bond + bonds - 1, bonds)
     has_lo, has_hi = f > 0, f < nf - 1
-    even = lax.rem(bond, 2) == 0
+    odd = lax.rem(bond, 2) == 1
+
+    half = d // 2
+
+    def cols(h):
+        return pl.ds(pl.multiple_of(h * half, half), half)
 
     def load(q):
         return pltpu.make_async_copy(left.at[q], left_v.at[q], lsem.at[q])
 
     small = [
         pltpu.make_async_copy(start, start_v, lsem.at[S]),
-        pltpu.make_async_copy(gate, gate_v, lsem.at[S + 1]),
-        pltpu.make_async_copy(sign, sign_v, lsem.at[S + 2]),
+        pltpu.make_async_copy(table, table_v, lsem.at[S + 1]),
     ]
 
-    def shift(q):
+    def shift(q, h):
         return pltpu.make_async_remote_copy(
-            src_ref=right.at[q], dst_ref=partner.at[q], send_sem=rs_sem.at[q],
-            recv_sem=rr_sem.at[q], device_id={"bond": behind}, device_id_type=MESH)
-
-    def up(q):
+            src_ref=right.at[q, :, cols(h)], dst_ref=partner.at[q, :, cols(h)],
+            send_sem=rs_sem.at[q, h], recv_sem=rr_sem.at[q, h],
+            device_id={"bond": behind}, device_id_type=MESH)
+
+    def up(q, h):
         return pltpu.make_async_remote_copy(
-            src_ref=pair.at[q], dst_ref=below.at[q], send_sem=ps_sem.at[0, q],
-            recv_sem=pr_sem.at[0, q], device_id={"sec": f + 1}, device_id_type=MESH)
-
-    def down(q):
+            src_ref=pair.at[q, :, cols(h)], dst_ref=below.at[q, :, cols(h)],
+            send_sem=ps_sem.at[0, q, h], recv_sem=pr_sem.at[0, q, h],
+            device_id={"sec": f + 1}, device_id_type=MESH)
+
+    def down(q, h):
         return pltpu.make_async_remote_copy(
-            src_ref=pair.at[q], dst_ref=above.at[q], send_sem=ps_sem.at[1, q],
-            recv_sem=pr_sem.at[1, q], device_id={"sec": f - 1}, device_id_type=MESH)
+            src_ref=pair.at[q, :, cols(h)], dst_ref=above.at[q, :, cols(h)],
+            send_sem=ps_sem.at[1, q, h], recv_sem=pr_sem.at[1, q, h],
+            device_id={"sec": f - 1}, device_id_type=MESH)
 
     def back(s):
         return pltpu.make_async_remote_copy(
             src_ref=out.at[s], dst_ref=right_new.at[s], send_sem=os_sem.at[s],
             recv_sem=or_sem.at[s], device_id={"bond": ahead}, device_id_type=MESH)
+
+    def both(act, where=True):
+        @pl.when(jnp.logical_and(where, has_hi))
+        def _():
+            act(up)
+
+        @pl.when(jnp.logical_and(where, has_lo))
+        def _():
+            act(down)
 
     barrier = pltpu.get_barrier_semaphore()
     pl.semaphore_signal(barrier, inc=1, device_id={"bond": ahead}, device_id_type=MESH)
@@ -130,7 +146,22 @@
         copy.start()
     pl.semaphore_wait(barrier, 2 + has_lo.astype(jnp.int32) + has_hi.astype(jnp.int32))
     for q in range(S):
-        shift(q).start()
+        for h in range(2):
+            shift(q, h).start()
+
+    def multiply(i, c):
+        q, h = i // 2, lax.rem(i, 2)
+
+        @pl.when(h == 0)
+        def _():
+            load(q).wait()
+
+        shift(q, h).wait_recv()
+        pair[q, :, cols(h)] = dot(left_v[q], partner[q, :, cols(h)], 1, 0).astype(BF)
+        both(lambda way: way(q, h).start(), jnp.logical_or(odd, q < S - 1))
+        return c
+
+    lax.fori_loop(0, 2 * S, multiply, 0)
 
     @pl.when(jnp.logical_not(has_lo))
     def _():
@@ -140,81 +171,52 @@
     def _():
         above[...] = jnp.zeros_like(above)
 
-    def multiply(q, c):
-        load(q).wait()
-        shift(q).wait_recv()
-
-        def rows(i, c):
-            at = pl.ds(pl.multiple_of(i * 128, 128), 128)
-            pair[q, at, :] = dot(left_v[q, at, :], partner[q], 1, 0).astype(BF)
-            return c
-
-        lax.fori_loop(0, d // 128, rows, 0)
-
-        @pl.when(jnp.logical_and(even, q == S - 1))
-        def _():
-            pl.semaphore_wait(turn, 1)
-
-        @pl.when(has_hi)
-        def _():
-            up(q).start()
-
-        @pl.when(has_lo)
-        def _():
-            down(q).start()
-
-        return c
-
-    lax.fori_loop(0, S, multiply, 0)
     for copy in small:
         copy.wait()
     for s in range(S):
         bt[s] = start_v[s].T
 
-    @pl.when(jnp.logical_not(even))
-    def _():
-        for q in range(S):
-            @pl.when(has_hi)
-            def _():
-                up(q).wait_send()
-
-            @pl.when(has_lo)
-            def _():
-                down(q).wait_send()
-
-        pl.semaphore_signal(turn, inc=1, device_id={"bond": behind}, device_id_type=MESH)
-
-
     firsts = (jnp.maximum(f - 1, 0), f, jnp.minimum(f + 1, nf - 1))
     here = (has_lo.astype(F32), None, has_hi.astype(F32))
 
-    def arrive(q):
+    def arrive(q, h):
         @pl.when(has_lo)
         def _():
-            up(q).wait_recv()
+            up(q, h).wait_recv()
 
         @pl.when(has_hi)
         def _():
-            down(q).wait_recv()
-
-    def mix(p):
+            down(q, h).wait_recv()
+
+    def mix(p, h):
         terms = []
         for first, gone, block in zip(firsts, here, (below, pair, above)):
             for q in range(max(0, p - 1), min(S, p + 2)):
-                row, column = f * S + p, first * S + q
-                w = gate_v[row, column] * (1.0 - 2.0 * sign_v[row, column].astype(F32))
+                w = table_v[f * S + p, first * S + q]
                 terms.append((w if gone is None else w * gone, block, q))
 
         def rows(i, c):
-            at = pl.ds(pl.multiple_of(i * 16, 16), 16)
+            at = pl.ds(pl.multiple_of(i * 32, 32), 32)
             total = None
             for w, block, q in terms:
-                term = w * block[q, at, :].astype(F32)
+                term = w * block[q, at, h * half:(h + 1) * half].astype(F32)
                 total = term if total is None else total + term
-            theta[p, at, :] = total.astype(BF)
+            theta[p, at, h * half:(h + 1) * half] = total.astype(BF)
             return c
 
-        lax.fori_loop(0, d // 16, rows, 0)
+        lax.fori_loop(0, d // 32, rows, 0)
+
+    def square(s, h):
+        for k in range(2):
+            part = slice(k * half, (k + 1) * half)
+            wide = slice(h * half, (h + 1) * half)
+            o = dot(theta[s, :, wide], theta[s, part, wide], 1, 1)
+            if h == 0:
+                total[s % 2, :, part] = o
+            else:
+                hi, lo = split2(total[s % 2, :, part] + o)
+                gram[s, 0, :, part] = hi
+                gram[s, 1, :, part] = lo
 
     def by_gram(s, x):
         h, m = split2(x)
@@ -233,28 +235,39 @@
         aug[s * n:(s + 1) * n, :] = (o[:n, :n] + o[n:, n:]) + (o[:n, n:] + o[n:, :n])
 
     def begin(s):
-        def rows(i, c):
-            at = pl.ds(pl.multiple_of(i * 128, 128), 128)
-            h, m = split2(dot(theta[s, at, :], theta[s], 1, 1))
-            gram[s, 0, at, :] = h
-            gram[s, 1, at, :] = m
-            return c
-
-        lax.fori_loop(0, d // 128, rows, 0)
+        for h in range(2):
+            mix(s, h)
+            square(s, h)
         put(s, by_gram(s, bt[s]))
 
-    arrive(0)
-    arrive(1)
-    mix(0)
+    for q in range(2):
+        for h in range(2):
+            arrive(q, h)
     begin(0)
-    arrive(2)
-    mix(1)
+
+    @pl.when(odd)
+    def _():
+        for q in range(S):
+            for h in range(2):
+                both(lambda way: way(q, h).wait_send())
+        pl.semaphore_signal(turn, inc=1, device_id={"bond": behind}, device_id_type=MESH)
+
+    @pl.when(jnp.logical_not(odd))
+    def _():
+        pl.semaphore_wait(turn, 1)
+        for h in range(2):
+            both(lambda way: way(S - 1, h).start())
+
+    for h in range(2):
+        arrive(2, h)
     begin(1)
-    arrive(3)
-    mix(2)
-    mix(3)
-    begin(2)
-    begin(3)
+    for h in range(2):
+        arrive(3, h)
+        for s in (2, 3):
+            mix(s, h)
+            square(s, h)
+    for s in (2, 3):
+        put(s, by_gram(s, bt[s]))
 
     def step(it, c):
         def meanwhile(t):
@@ -271,45 +284,38 @@
         return c
 
     lax.fori_loop(0, ITERS, step, 0)
-    row = lax.broadcasted_iota(jnp.int32, (n, d), 0)
+    row = lax.broadcasted_iota(jnp.int32, (n, d), 0).astype(F32)
     for s in range(S):
-        masked = jnp.where(row < kept[0, s], by_tri(s, gt[s]), 0.0)
+        masked = jnp.where(row < table_v[nf * S, s], by_tri(s, gt[s]), 0.0)
         bt[s] = masked
         out[s] = sum_rows(dot(jnp.concatenate(split2(masked), axis=0), theta[s], 1, 0), n).astype(BF)
         back(s).start()
     for s in range(S):
         left_new[s] = bt[s].T.astype(BF)
     for q in range(S):
-        shift(q).wait_send()
-
-        @pl.when(jnp.logical_and(even, has_hi))
-        def _():
-            up(q).wait_send()
-
-        @pl.when(jnp.logical_and(even, has_lo))
-        def _():
-            down(q).wait_send()
+        for h in range(2):
+            shift(q, h).wait_send()
+            both(lambda way: way(q, h).wait_send(), jnp.logical_not(odd))
 
     for s in range(S):
         back(s).wait()
 
 
-def layer(left, right, gate, sign, kept, start):
+def layer(left, right, table, start):
     S, d, n = start.shape
     block = pltpu.VMEM((S, d, d), BF)
     dma = pltpu.SemaphoreType.DMA
     hbm = pl.BlockSpec(memory_space=pltpu.HBM)
-    smem = pl.BlockSpec(memory_space=pltpu.SMEM)
     return pl.pallas_call(
         layer_body,
         out_shape=(jax.ShapeDtypeStruct((S, d, n), BF), jax.ShapeDtypeStruct((S, n, d), BF)),
-        in_specs=[hbm, hbm, hbm, hbm, smem, hbm],
+        in_specs=[hbm] * 4,
         out_specs=[pl.BlockSpec(memory_space=pltpu.VMEM), pl.BlockSpec(memory_space=pl.ANY)],
         scratch_shapes=[block] * 6 + [
+            pltpu.VMEM((2, d, d), F32),
             pltpu.VMEM((S, 2, d, d), BF),
             pltpu.VMEM((S, d, n), F32),
-            pltpu.SMEM(gate.shape, F32),
-            pltpu.SMEM(sign.shape, jnp.int32),
+            pltpu.SMEM(table.shape, F32),
             pltpu.VMEM((S, n, d), F32),
             pltpu.VMEM((S, n, d), F32),
             pltpu.VMEM((S, n, d), F32),
@@ -318,16 +324,19 @@
             pltpu.VMEM((S * NB, n), F32),
             pltpu.VMEM((S * n, n), F32),
             pltpu.VMEM((S, n, d), BF),
-            dma((S + 3,)), dma((S,)), dma((S,)), dma((2, S)), dma((2, S)), dma((S,)), dma((S,)),
+            dma((S + 2,)), dma((S, 2)), dma((S, 2)), dma((2, S, 2)), dma((2, S, 2)), dma((S,)), dma((S,)),
             pltpu.SemaphoreType.REGULAR,
         ],
         compiler_params=pltpu.CompilerParams(
             collective_id=0, has_side_effects=True, vmem_limit_bytes=52 * 2**20),
-    )(left, right, gate, sign, kept, start)
+    )(left, right, table, start)
 
 
 def shards(left_site, right_site, gate, sign_table, kept, start):
-    left_new, right_new = layer(left_site[0], right_site[0], gate, sign_table, kept, start[0])
+    coef = gate * (1.0 - 2.0 * sign_table.astype(F32))
+    counts = jnp.pad(kept.astype(F32), ((0, 0), (0, gate.shape[1] - kept.shape[1])))
+    table = jnp.concatenate([coef, counts], axis=0)
+    left_new, right_new = layer(left_site[0], right_site[0], table, start[0])
     return left_new[None], right_new[None]
 
 

time: 98.7 us -> 91.2 us (0.924)
  Pallas kernels: 94.1 us -> 87.4 us
  local copies, waits for them, and re-layouts: 3.75 us -> 1.59 us
  other arithmetic: 0 us -> 1.45 us
    pallas_call x1, Pallas kernels: 94.1 us -> 87.4 us  [layer(): pl.pallas_call(layer_body, out_shape=(jax.ShapeDtypeStruct((S, d, n), BF)...]
    unnamed x8 -> x2, local copies, waits for them, and re-layouts: 3.75 us -> 1.59 us
where the time goes in v5:
time: 91.2 us; the launch traced here: 91.1 us
  Pallas kernels  87.4 us (96%)
  local copies, waits for them, and re-layouts  1.59 us (2%)
  other arithmetic  1.45 us (2%)
    pallas_call x1, Pallas kernels, layer(): pl.pallas_call(layer_body, out_shape=(jax.ShapeDtypeStruct((S, d, n), BF)...  87.4 us

profile of v5, /device:TPU:24, one launch (start us, length us, event | category | flops | bytes accessed | tf_op | source)
XLA Modules:
  0.0 91.1 jit_solution(10213289195626816912)
XLA Ops:
  0.6 0.7 convert_element_type.9
  1.3 0.8 subtract_multiply_fusion
  2.1 87.4 %shard_map.77 = (bf16[4,512,128]{2,1,0:T(8,128)(2,1)S(1)}, bf16[4,128,512]{2,1,0:T(8,128)(2,1)S(1)}) custom-call(bf16[4,512,512]{2,1,0:T(8,128)(2,1)} %bitcast.7, bf16[4,512,512]{2,1,0:T(8,128)(2,1)} %bitcast.8, f32[65,64]{1,0:T(8,128)S(1)} %select_maximum_fusion.table, f32[4,512,128]{2,1,0:T(8,128)} %bitcast.9), custom_call_target="tpu_custom_call" | custom-call | tf_op jit(solution)/shard_map/pallas_call | solution.py:309
  89.5 0.8 copy.10
  90.3 0.8 copy.11
  (1 shorter events, 0.0 us)

commit v6 on v5

--- a/solution.py
+++ b/solution.py
@@ -35,17 +35,18 @@
     for t in range(n//nb):
         lo=t*nb; end=lo+nb
         v={(i,k):bc(X[i],lo+k) for k in range(nb) for i in range(k,nb)}
+        X=[jnp.where(within(lo,end),0.0,x) for x in X]
         for j in range(nb):
             r=lax.rsqrt(v[j,j])
             U=jnp.where(lane==lo+j,r,X[j]*r)
             tri[pl.ds(lo+j,S,stride=n),:]=jnp.where(lane<=lo+j,U,0.0)
             if end<n:
-                ubuf[pl.ds(j,S,stride=nb),:]=jnp.where(within(lo+j+1,end),0.0,U) if j<nb-1 else U
+                ubuf[pl.ds(j,S,stride=nb),:]=U
             col={i:v[i,j]*r for i in range(j+1,nb)}
             for i in range(j+1,nb):
                 for k in range(j+1,i+1):
                     v[i,k]=v[i,k]-col[i]*col[k]
-                X[i]=jnp.where(lane==lo+j,0.0,X[i])-col[i]*U
+                X[i]=X[i]-col[i]*U
         if end<n:
             blk=jnp.logical_and(lane1>=lo,lane1<end)
             lt,rh=[],[]
@@ -158,7 +159,7 @@
 
         shift(q, h).wait_recv()
         pair[q, :, cols(h)] = dot(left_v[q], partner[q, :, cols(h)], 1, 0).astype(BF)
-        both(lambda way: way(q, h).start(), jnp.logical_or(odd, q < S - 1))
+        both(lambda way: way(q, h).start(), jnp.logical_or(odd, i < 2 * S - 4))
         return c
 
     lax.fori_loop(0, 2 * S, multiply, 0)
@@ -224,8 +225,8 @@
                 + dot(h, gram[s, 1], 1, 0))
 
     def by_tri(s, x):
-        a, b, l = split3(tri[s * n:(s + 1) * n, :])
-        lhs = jnp.concatenate([jnp.concatenate([y, y], axis=1) for y in (a, b, l)], axis=0)
+        a, b = split2(tri[s * n:(s + 1) * n, :])
+        lhs = jnp.concatenate([jnp.concatenate([y, y], axis=1) for y in (a, b)], axis=0)
         return sum_rows(dot(lhs, jnp.concatenate(split2(x), axis=0), 1, 0), n)
 
     def put(s, g):
@@ -247,16 +248,16 @@
 
     @pl.when(odd)
     def _():
-        for q in range(S):
-            for h in range(2):
-                both(lambda way: way(q, h).wait_send())
-        pl.semaphore_signal(turn, inc=1, device_id={"bond": behind}, device_id_type=MESH)
+        for i in range(2 * S):
+            if i == 2 * S - 1:
+                pl.semaphore_signal(turn, inc=1, device_id={"bond": behind}, device_id_type=MESH)
+            both(lambda way: way(i // 2, i % 2).wait_send())
 
     @pl.when(jnp.logical_not(odd))
     def _():
         pl.semaphore_wait(turn, 1)
-        for h in range(2):
-            both(lambda way: way(S - 1, h).start())
+        for i in range(2 * S - 4, 2 * S):
+            both(lambda way: way(i // 2, i % 2).start())
 
     for h in range(2):
         arrive(2, h)

time: 91.2 us -> 87.5 us (0.959)
  Pallas kernels: 87.4 us -> 83.1 us
    pallas_call x1, Pallas kernels: 87.4 us -> 83.1 us  [layer(): pl.pallas_call(layer_body, out_shape=(jax.ShapeDtypeStruct((S, d, n), BF)...]
where the time goes in v6:
time: 87.5 us; the launch traced here: 86.8 us
  Pallas kernels  83.1 us (95%)
  local copies, waits for them, and re-layouts  1.59 us (2%)
  other arithmetic  1.45 us (2%)
    pallas_call x1, Pallas kernels, layer(): pl.pallas_call(layer_body, out_shape=(jax.ShapeDtypeStruct((S, d, n), BF)...  83.1 us

profile of v6, /device:TPU:24, one launch (start us, length us, event | category | flops | bytes accessed | tf_op | source)
XLA Modules:
  0.0 86.8 jit_solution(5749256927032660974)
XLA Ops:
  0.6 0.7 convert_element_type.9
  1.3 0.8 subtract_multiply_fusion
  2.1 83.1 %shard_map.77 = (bf16[4,512,128]{2,1,0:T(8,128)(2,1)S(1)}, bf16[4,128,512]{2,1,0:T(8,128)(2,1)S(1)}) custom-call(bf16[4,512,512]{2,1,0:T(8,128)(2,1)} %bitcast.7, bf16[4,512,512]{2,1,0:T(8,128)(2,1)} %bitcast.8, f32[65,64]{1,0:T(8,128)S(1)} %select_maximum_fusion.table, f32[4,512,128]{2,1,0:T(8,128)} %bitcast.9), custom_call_target="tpu_custom_call" | custom-call | tf_op jit(solution)/shard_map/pallas_call | solution.py:310
  85.2 0.8 copy.10
  86.0 0.8 copy.11
  (1 shorter events, 0.0 us)

commit v7 on v6

--- a/solution.py
+++ b/solution.py
@@ -1,4 +1,3 @@
-import functools
 import jax
 import jax.numpy as jnp
 from jax import lax
@@ -23,47 +22,99 @@
     return h, (x - h.astype(F32)).astype(BF)
 
 
-def dot(a,b,ca,cb):
-    return lax.dot_general(a,b,(((ca,),(cb,)),((),())),preferred_element_type=F32)
+def dot(a, b, ca, cb):
+    return lax.dot_general(a, b, (((ca,), (cb,)), ((), ())), preferred_element_type=F32)
+
 
 def factor(aug, ubuf, nbuf, tri, n, S, nb, hook):
-    lane=lax.broadcasted_iota(jnp.int32,(S,n),1)
-    lane1=lax.broadcasted_iota(jnp.int32,(1,n),1)
-    def bc(x,i): return jnp.broadcast_to(x[:,i:i+1],(S,n))
-    def within(a,b): return jnp.logical_and(lane>=a,lane<b)
-    X=[aug[pl.ds(k,S,stride=n),:] for k in range(nb)]
-    for t in range(n//nb):
-        lo=t*nb; end=lo+nb
-        v={(i,k):bc(X[i],lo+k) for k in range(nb) for i in range(k,nb)}
-        X=[jnp.where(within(lo,end),0.0,x) for x in X]
-        for j in range(nb):
-            r=lax.rsqrt(v[j,j])
-            U=jnp.where(lane==lo+j,r,X[j]*r)
-            tri[pl.ds(lo+j,S,stride=n),:]=jnp.where(lane<=lo+j,U,0.0)
-            if end<n:
-                ubuf[pl.ds(j,S,stride=nb),:]=U
-            col={i:v[i,j]*r for i in range(j+1,nb)}
-            for i in range(j+1,nb):
-                for k in range(j+1,i+1):
-                    v[i,k]=v[i,k]-col[i]*col[k]
-                X[i]=X[i]-col[i]*U
-        if end<n:
-            blk=jnp.logical_and(lane1>=lo,lane1<end)
-            lt,rh=[],[]
+    lane = lax.broadcasted_iota(jnp.int32, (2 * S, n), 1)
+    lane1 = lax.broadcasted_iota(jnp.int32, (1, n), 1)
+    top = nb // 2
+
+    def spread(x, i):
+        return jnp.broadcast_to(x[:, i:i + 1], x.shape)
+
+    upper = lax.broadcasted_iota(jnp.int32, (2 * S, n), 0) < S
+
+    def update(z, low, first):
+        for k in range(first, top // 2):
+            cross = jnp.concatenate([low[k][S:], low[k][:S]], axis=0)
+            for p in range(k, top // 2):
+                z[p, k] = z[p, k][0] - low[p] * low[k], z[p, k][1] - low[p] * cross
+
+    def dup(x, h):
+        part = x[h * S:(h + 1) * S]
+        return jnp.concatenate([part, part], axis=0)
+
+    X = [aug[pl.ds(k, S, stride=n), :] for k in range(nb)]
+    for t in range(n // nb):
+        lo = t * nb
+        end = lo + nb
+        inside = jnp.logical_and(lane >= lo, lane < end)
+        XD = [jnp.concatenate([X[i], X[i]], axis=0) for i in range(top)]
+        XP = [jnp.concatenate([X[top + 2 * p], X[top + 2 * p + 1]], axis=0) for p in range(top // 2)]
+        v, w, z = {}, {}, {}
+        for k in range(top):
+            for i in range(k, top):
+                v[i, k] = spread(XD[i], lo + k)
+            for p in range(top // 2):
+                w[p, k] = spread(XP[p], lo + k)
+        for k in range(top // 2):
+            for p in range(k, top // 2):
+                one, two = spread(XP[p], lo + top + 2 * k), spread(XP[p], lo + top + 2 * k + 1)
+                z[p, k] = jnp.where(upper, one, two), jnp.where(upper, two, one)
+        XD = [jnp.where(inside, 0.0, x) for x in XD]
+        XP = [jnp.where(inside, 0.0, x) for x in XP]
+
+        def keep(j, u):
+            tri[pl.ds(lo + j, S, stride=n), :] = jnp.where(lane <= lo + j, u, 0.0)[:S]
+            if end < n:
+                ubuf[pl.ds(j, S, stride=nb), :] = u[:S]
+
+        for j in range(top):
+            r = lax.rsqrt(v[j, j])
+            u = jnp.where(lane == lo + j, r, XD[j] * r)
+            keep(j, u)
+            col = {i: v[i, j] * r for i in range(j + 1, top)}
+            low = [w[p, j] * r for p in range(top // 2)]
+            for i in range(j + 1, top):
+                for k in range(j + 1, i + 1):
+                    v[i, k] = v[i, k] - col[i] * col[k]
+                XD[i] = XD[i] - col[i] * u
+            for k in range(j + 1, top):
+                for p in range(top // 2):
+                    w[p, k] = w[p, k] - low[p] * col[k]
+            update(z, low, 0)
+            for p in range(top // 2):
+                XP[p] = XP[p] - low[p] * u
+        for j in range(top):
+            q, h = j // 2, j % 2
+            r = dup(lax.rsqrt(z[q, q][0]), h)
+            u = jnp.where(lane == lo + top + j, r, dup(XP[q], h) * r)
+            keep(top + j, u)
+            low = {p: jnp.where(upper, z[p, q][h], z[p, q][1 - h]) * r for p in range(q + h, top // 2)}
+            update(z, low, q + h)
+            for p in low:
+                XP[p] = XP[p] - low[p] * u
+        if end < n:
+            blk = jnp.logical_and(lane1 >= lo, lane1 < end)
+            lt, rh = [], []
             for s in range(S):
-                h,m,l=split3(ubuf[s*nb:(s+1)*nb,:])
-                lt.append(jnp.concatenate([h,h,m,h,m,l],axis=0).T)
-                rh.append(jnp.concatenate([h,m,h,l,m,h],axis=0))
-            o=dot(jnp.concatenate([x[end:end+nb] for x in lt],axis=0),jnp.concatenate(rh,axis=1),1,0)
+                h, m, l = split3(ubuf[s * nb:(s + 1) * nb, :])
+                lt.append(jnp.concatenate([h, h, m, h, m, l], axis=0).T)
+                rh.append(jnp.concatenate([h, m, h, l, m, h], axis=0))
+            o = dot(jnp.concatenate([x[end:end + nb] for x in lt], axis=0), jnp.concatenate(rh, axis=1), 1, 0)
             for s in range(S):
-                nbuf[s*nb:(s+1)*nb,:]=jnp.where(blk,0.0,aug[s*n+end:s*n+end+nb,:])-o[s*nb:(s+1)*nb,s*n:(s+1)*n]
-            X=[nbuf[pl.ds(k,S,stride=nb),:] for k in range(nb)]
-            first=end+nb
+                nbuf[s * nb:(s + 1) * nb, :] = (
+                    jnp.where(blk, 0.0, aug[s * n + end:s * n + end + nb, :])
+                    - o[s * nb:(s + 1) * nb, s * n:(s + 1) * n])
+            X = [nbuf[pl.ds(k, S, stride=nb), :] for k in range(nb)]
             hook(t)
-            if first<n:
+            if end + nb < n:
                 for s in range(S):
-                    rows=slice(s*n+first,(s+1)*n)
-                    aug[rows,:]=jnp.where(blk,0.0,aug[rows,:])-dot(lt[s][first:],rh[s],1,0)
+                    rows = slice(s * n + end + nb, (s + 1) * n)
+                    aug[rows, :] = jnp.where(blk, 0.0, aug[rows, :]) - dot(lt[s][end + nb:], rh[s], 1, 0)
+
 
 def sum_rows(x, n):
     total = x[:n]

time: 87.5 us -> 84.9 us (0.970)
  Pallas kernels: 83.1 us -> 80.5 us
    pallas_call x1, Pallas kernels: 83.1 us -> 80.5 us  [layer(): pl.pallas_call(layer_body, out_shape=(jax.ShapeDtypeStruct((S, d, n), BF)...]
where the time goes in v7:
time: 84.9 us; the launch traced here: 84.2 us
  Pallas kernels  80.5 us (95%)
  local copies, waits for them, and re-layouts  1.59 us (2%)
  other arithmetic  1.45 us (2%)
    pallas_call x1, Pallas kernels, layer(): pl.pallas_call(layer_body, out_shape=(jax.ShapeDtypeStruct((S, d, n), BF)...  80.5 us

profile of v7, /device:TPU:24, one launch (start us, length us, event | category | flops | bytes accessed | tf_op | source)
XLA Modules:
  0.0 84.2 jit_solution(14056000846977755374)
XLA Ops:
  0.6 0.7 convert_element_type.9
  1.3 0.8 subtract_multiply_fusion
  2.1 80.5 %shard_map.77 = (bf16[4,512,128]{2,1,0:T(8,128)(2,1)S(1)}, bf16[4,128,512]{2,1,0:T(8,128)(2,1)S(1)}) custom-call(bf16[4,512,512]{2,1,0:T(8,128)(2,1)} %bitcast.7, bf16[4,512,512]{2,1,0:T(8,128)(2,1)} %bitcast.8, f32[65,64]{1,0:T(8,128)S(1)} %select_maximum_fusion.table, f32[4,512,128]{2,1,0:T(8,128)} %bitcast.9), custom_call_target="tpu_custom_call" | custom-call | tf_op jit(solution)/shard_map/pallas_call | solution.py:361
  82.6 0.8 copy.10
  83.4 0.8 copy.11
  (1 shorter events, 0.0 us)

commit v8 on v7

--- a/solution.py
+++ b/solution.py
@@ -103,11 +103,10 @@
                 h, m, l = split3(ubuf[s * nb:(s + 1) * nb, :])
                 lt.append(jnp.concatenate([h, h, m, h, m, l], axis=0).T)
                 rh.append(jnp.concatenate([h, m, h, l, m, h], axis=0))
-            o = dot(jnp.concatenate([x[end:end + nb] for x in lt], axis=0), jnp.concatenate(rh, axis=1), 1, 0)
             for s in range(S):
                 nbuf[s * nb:(s + 1) * nb, :] = (
                     jnp.where(blk, 0.0, aug[s * n + end:s * n + end + nb, :])
-                    - o[s * nb:(s + 1) * nb, s * n:(s + 1) * n])
+                    - dot(lt[s][end:end + nb], rh[s], 1, 0))
             X = [nbuf[pl.ds(k, S, stride=nb), :] for k in range(nb)]
             hook(t)
             if end + nb < n:

time: 84.9 us -> 84.3 us (level)
  no operation moved by 1% of the time
where the time goes in v8:
time: 84.3 us; the launch traced here: 83.6 us
  Pallas kernels  80 us (95%)
  local copies, waits for them, and re-layouts  1.59 us (2%)
  other arithmetic  1.45 us (2%)
    pallas_call x1, Pallas kernels, layer(): pl.pallas_call(layer_body, out_shape=(jax.ShapeDtypeStruct((S, d, n), BF)...  80 us

profile of v8, /device:TPU:24, one launch (start us, length us, event | category | flops | bytes accessed | tf_op | source)
XLA Modules:
  0.0 83.6 jit_solution(16946045447285667929)
XLA Ops:
  0.6 0.7 convert_element_type.9
  1.3 0.8 subtract_multiply_fusion
  2.1 80.0 %shard_map.77 = (bf16[4,512,128]{2,1,0:T(8,128)(2,1)S(1)}, bf16[4,128,512]{2,1,0:T(8,128)(2,1)S(1)}) custom-call(bf16[4,512,512]{2,1,0:T(8,128)(2,1)} %bitcast.7, bf16[4,512,512]{2,1,0:T(8,128)(2,1)} %bitcast.8, f32[65,64]{1,0:T(8,128)S(1)} %select_maximum_fusion.table, f32[4,512,128]{2,1,0:T(8,128)} %bitcast.9), custom_call_target="tpu_custom_call" | custom-call | tf_op jit(solution)/shard_map/pallas_call | solution.py:360
  82.0 0.8 copy.10
  82.8 0.8 copy.11
  (1 shorter events, 0.0 us)

commit v9 on v8

--- a/solution.py
+++ b/solution.py
@@ -123,7 +123,7 @@
 
 
 def layer_body(left, right, table, start, left_new, right_new,
-               left_v, partner, pair, below, above, theta, total, gram, start_v, table_v,
+               left_v, partner, pair, below, above, theta, partial, total, gram, start_v, table_v,
                bt, gt, ht, aug, ubuf, nbuf, tri, out,
                lsem, rs_sem, rr_sem, ps_sem, pr_sem, os_sem, or_sem, turn):
     S, d, _ = left_v.shape
@@ -239,20 +239,27 @@
         def _():
             down(q, h).wait_recv()
 
-    def mix(p, h):
+    def mix(p, h, early=False, late=False):
         terms = []
         for first, gone, block in zip(firsts, here, (below, pair, above)):
             for q in range(max(0, p - 1), min(S, p + 2)):
+                last = q == S - 1 and gone is not None
+                if (early and last) or (late and not last):
+                    continue
                 w = table_v[f * S + p, first * S + q]
                 terms.append((w if gone is None else w * gone, block, q))
+        wide = slice(h * half, (h + 1) * half)
 
         def rows(i, c):
             at = pl.ds(pl.multiple_of(i * 32, 32), 32)
-            total = None
+            value = partial[p % 2, at, wide] if late else None
             for w, block, q in terms:
-                term = w * block[q, at, h * half:(h + 1) * half].astype(F32)
-                total = term if total is None else total + term
-            theta[p, at, h * half:(h + 1) * half] = total.astype(BF)
+                term = w * block[q, at, wide].astype(F32)
+                value = term if value is None else value + term
+            if early:
+                partial[p % 2, at, wide] = value
+            else:
+                theta[p, at, wide] = value.astype(BF)
             return c
 
         lax.fori_loop(0, d // 32, rows, 0)
@@ -313,9 +320,12 @@
         arrive(2, h)
     begin(1)
     for h in range(2):
+        for s in (2, 3):
+            mix(s, h, early=True)
+    for h in range(2):
         arrive(3, h)
         for s in (2, 3):
-            mix(s, h)
+            mix(s, h, late=True)
             square(s, h)
     for s in (2, 3):
         put(s, by_gram(s, bt[s]))
@@ -363,6 +373,7 @@
         in_specs=[hbm] * 4,
         out_specs=[pl.BlockSpec(memory_space=pltpu.VMEM), pl.BlockSpec(memory_space=pl.ANY)],
         scratch_shapes=[block] * 6 + [
+            pltpu.VMEM((2, d, d), F32),
             pltpu.VMEM((2, d, d), F32),
             pltpu.VMEM((S, 2, d, d), BF),
             pltpu.VMEM((S, d, n), F32),

time: 84.3 us -> 83.8 us (level)
  no operation moved by 1% of the time
where the time goes in v9:
time: 83.8 us; the launch traced here: 83.1 us
  Pallas kernels  79.4 us (95%)
  local copies, waits for them, and re-layouts  1.59 us (2%)
  other arithmetic  1.45 us (2%)
    pallas_call x1, Pallas kernels, layer(): pl.pallas_call(layer_body, out_shape=(jax.ShapeDtypeStruct((S, d, n), BF)...  79.4 us

profile of v9, /device:TPU:24, one launch (start us, length us, event | category | flops | bytes accessed | tf_op | source)
XLA Modules:
  0.0 83.1 jit_solution(5346057446318869442)
XLA Ops:
  0.6 0.7 convert_element_type.9
  1.3 0.8 subtract_multiply_fusion
  2.1 79.4 %shard_map.77 = (bf16[4,512,128]{2,1,0:T(8,128)(2,1)S(1)}, bf16[4,128,512]{2,1,0:T(8,128)(2,1)S(1)}) custom-call(bf16[4,512,512]{2,1,0:T(8,128)(2,1)} %bitcast.7, bf16[4,512,512]{2,1,0:T(8,128)(2,1)} %bitcast.8, f32[65,64]{1,0:T(8,128)S(1)} %select_maximum_fusion.table, f32[4,512,128]{2,1,0:T(8,128)} %bitcast.9), custom_call_target="tpu_custom_call" | custom-call | tf_op jit(solution)/shard_map/pallas_call | solution.py:370
  81.5 0.8 copy.10
  82.3 0.8 copy.11
  (1 shorter events, 0.0 us)
